TPU v7x, 256 devices: a whole 4x4x8 slice. The times are simulated.
256 devices in a mesh: span: 16 (over z, x_hi), mp: 16 (over y, x_lo, core).
Axes of the slice: x: 4 (x_hi: 2, x_lo: 2; x = x_hi * 2 + x_lo), y: 4, z: 8, core: 2. Of those that a mesh axis runs over, the one named last changes fastest.
Arguments:
- queries: bfloat16 [12288, 6144], P('span', 'mp'), may hold values from -11 to 11
- keys: bfloat16 [12288, 6144], P('span', 'mp'), may hold values from -11 to 11
- values: bfloat16 [12288, 6144], P('span', 'mp'), may hold values from -6 to 6
- residual: bfloat16 [12288, 6144], P(('span', 'mp')), may hold values from -6 to 6
- out_weight: bfloat16 [6144, 6144], P('mp'), may hold values from -0.078125 to 0.078125
- gate_table: float32 [16, 6144], replicated, may hold values from 0.5 to 2
- noise_steps: int32 [16], replicated, may hold values from 0 to 15, each once
- windows: int32 [16, 2], replicated, may hold values 0 or 1
Outputs:
- mixed: bfloat16 [12288, 6144], P(('span', 'mp'))
All inputs are finite; a program needn't handle non-finite values.
Results may differ from a plain program's by a relative error of at most 0.018.
Values may be sent and summed in bfloat16 or wider, within the bound.
No kernel may reach another device: no remote copies, remote signals or barrier semaphores. Data moves between devices by JAX's collectives and lax.ppermute only.
A program may use at most 64 MiB of HBM per device.

v0:
```python
import jax
import jax.numpy as jnp
from jax import lax
from jax.sharding import PartitionSpec as P

HD = 128
LAGS = 2


def spread(value, axis, source):
    kept = jnp.where(lax.axis_index(axis) == source, value, 0).astype(value.dtype)
    return lax.psum(kept, axis)


def from_behind(value, axis, steps):
    count = lax.axis_size(axis)
    pairs = [(source, (source + steps) % count) for source in range(count)]
    return lax.ppermute(value, axis, pairs)


def attend_head(query_rows, key_rows, value_rows, key_live):
    scores = jnp.dot(query_rows, key_rows.T, preferred_element_type=jnp.float32) * HD ** (-0.5)
    scores = jnp.where(key_live[None, :], scores, -1e30)
    row_peak = jnp.max(scores, axis=1, keepdims=True)
    exp_scores = jnp.exp(scores - row_peak)
    weights_bf = (exp_scores / jnp.sum(exp_scores, axis=1, keepdims=True)).astype(jnp.bfloat16)
    return jnp.dot(weights_bf, value_rows, preferred_element_type=jnp.float32).astype(jnp.bfloat16)


def local(queries, keys, values, residual, out_weight, gate_table, noise_steps, windows):
    groups = lax.axis_size("span")
    my_span = lax.axis_index("span")
    span_rows = queries.shape[0]
    span_ids = lax.iota(jnp.int32, groups)
    clean_root = jnp.sum(span_ids * (noise_steps == 0).astype(jnp.int32))
    kv_cache = jnp.stack([keys, values])
    clean = spread(kv_cache, "span", clean_root)
    key_parts = [keys, clean[0]]
    value_parts = [values, clean[1]]
    live_flags = [jnp.array(True), my_span != clean_root]
    for lag_index in range(LAGS):
        received = from_behind(kv_cache, "span", lag_index + 1)
        key_parts.append(received[0])
        value_parts.append(received[1])
        live_flags.append(windows[my_span, lag_index] == 1)
    all_keys = jnp.concatenate(key_parts, 0)
    all_values = jnp.concatenate(value_parts, 0)
    key_live = jnp.concatenate([jnp.broadcast_to(flag, (span_rows,)) for flag in live_flags])
    heads_here = queries.shape[1] // HD
    head_outputs = []
    for head_index in range(heads_here):
        lower = head_index * HD
        head_outputs.append(
            attend_head(
                queries[:, lower : lower + HD],
                all_keys[:, lower : lower + HD],
                all_values[:, lower : lower + HD],
                key_live,
            )
        )
    attended = jnp.concatenate(head_outputs, axis=1)
    head_terms = jnp.dot(attended, out_weight, preferred_element_type=jnp.float32)
    summed = lax.psum_scatter(
        head_terms.astype(jnp.bfloat16), "mp", scatter_dimension=0, tiled=True
    ).astype(jnp.float32)
    selector = (span_ids == noise_steps[my_span]).astype(jnp.float32)
    gate_row = jnp.dot(selector, gate_table, precision=lax.Precision.HIGHEST)
    return (residual.astype(jnp.float32) + gate_row[None, :] * summed).astype(jnp.bfloat16)


def solution(mesh):
    in_specs = (
        P("span", "mp"),
        P("span", "mp"),
        P("span", "mp"),
        P(("span", "mp"), None),
        P("mp", None),
        P(),
        P(),
        P(),
    )
    out_specs = P(("span", "mp"), None)
    return jax.shard_map(local, mesh=mesh, in_specs=in_specs, out_specs=out_specs, check_vma=False)
```

profile of v0, /device:TPU:24, one launch (start us, length us, event | category | flops | bytes accessed | tf_op | source)
XLA Modules:
  0.0 353.9 jit_solution(15241135134249096652)
XLA Ops:
  6.5 1.4 fusion.32
  8.5 2.9 broadcast_select_fusion
  11.5 3.0 collective-permute-start
  14.5 1.9 collective-permute-start.1
  17.1 0.7 constant_dynamic-slice_fusion.1
  19.2 29.2 %collective-permute-done = bf16[2,768,384]{2,1,0:T(8,128)(2,1)S(1)} collective-permute-done((bf16[2,768,384]{2,1,0:T(8,128)(2,1)}, bf16[2,768,384]{2,1,0:T(8,128)(2,1)S(1)}, u32[]{:S(2)}, u32[]{:S(2)}) %collective-permute-start) | collective-permute-done | bytes 1179680 | tf_op jit(solution)/shard_map/ppermute | solution.py:18
  48.6 1.4 slice_bitcast_fusion
  49.9 143.2 %all-reduce.2.cloned.1.call-done = bf16[2,768,384]{2,1,0:T(8,128)(2,1)} async-done(((bf16[2,768,384]{2,1,0:T(8,128)(2,1)}), bf16[2,768,384]{2,1,0:T(8,128)(2,1)}) %all-reduce.2.cloned.1.call-update) | async-done | bytes 1179664 | tf_op jit(solution)/shard_map/psum | solution.py:12
  193.1 1.4 slice_bitcast_fusion.2
  194.5 10.6 %pad_maximum_fusion = (bf16[3072,384]{1,0:T(8,128)(2,1)S(1)}, bf16[3072,384]{1,0:T(8,128)(2,1)}) fusion(bf16[768,384]{1,0:T(8,128)(2,1)S(1)} %get-tuple-element.15, bf16[768,384]{1,0:T(8,128)(2,1)S(1)} %get-tuple-element.13, bf16[768,384]{1,0:T(8,128)(2,1)S(1)} %get-tuple-element.11, bf16[768,384]{1,0:T(8,128)(2,1)} %param.9, ...), kind=kLoop, calls=%fused_computation.19 | loop fusion | flops 18874368 | bytes 9437184 | tf_op jit(solution)/shard_map/concatenate | solution.py:46
  205.1 1.4 fusion.13
  206.5 1.6 fusion
  208.1 8.3 %fusion.3 = (f32[768]{0:T(1024)S(1)}, f32[768]{0:T(1024)S(1)}, f32[768]{0:T(1024)S(1)}, f32[3072,768]{1,0:T(8,128)}) fusion(f32[3072,768]{1,0:T(8,128)S(1)} %get-tuple-element.21, f32[768]{0:T(1024)S(1)} %get-tuple-element.20, pred[3072]{0:T(1024)(128)(4,1)S(1)} %pad_add_fusion, f32[3072,768]{1,0:T(8,128)S(1)} %fusion.13, bf16[768,384]{1,0:T(8,128)(2,1)} %param.8, ...), kind=kOutput, calls=%fused_computation.13 | convolution fusion | flops 627570432 | bytes 29310976 | tf_op jit(solution)/shard_map/dot_general | solution.py:22
  216.5 3.1 fusion.11
  219.6 0.3 slice-done.1
  220.1 4.0 %fusion.4 = (f32[768]{0:T(1024)S(1)}, f32[768]{0:T(1024)S(1)}) fusion(f32[3072,768]{1,0:T(8,128)S(1)} %bitcast.24, f32[768]{0:T(1024)S(1)} %get-tuple-element.6, pred[3072]{0:T(1024)(128)(4,1)S(1)} %pad_add_fusion, f32[768]{0:T(1024)S(1)} %get-tuple-element.7, f32[3072,768]{1,0:T(8,128)S(1)} %fusion.13), kind=kLoop, calls=%fused_computation.14 | loop fusion | flops 18872832 | bytes 18889728 | tf_op jit(solution)/shard_map/reduce_sum | solution.py:26
  224.2 3.1 fusion.10
  227.3 3.1 fusion.9
  230.4 7.6 %convolution_convert_fusion = bf16[768,6144]{1,0:T(8,128)(2,1)} fusion(bf16[384,6144]{1,0:T(8,128)(2,1)S(1)} %bitcast.29, bf16[768,128]{1,0:T(8,128)(2,1)S(1)} %fusion.9, bf16[768,128]{1,0:T(8,128)(2,1)S(1)} %fusion.10, bf16[768,128]{1,0:T(8,128)(2,1)S(1)} %fusion.11), kind=kOutput, calls=%fused_computation | convolution fusion | flops 3630366720 | bytes 14745600 | tf_op jit(solution)/shard_map/dot_general | solution.py:62
  238.0 0.6 copy-done.6
  238.6 0.6 dynamic_slice.9
  239.2 0.9 fusion.29
  240.1 104.9 %reduce-scatter.2.cloned.1.call-done = bf16[48,6144]{1,0:T(8,128)(2,1)} async-done(((bf16[768,6144]{1,0:T(8,128)(2,1)}), bf16[48,6144]{1,0:T(8,128)(2,1)}) %reduce-scatter.2.cloned.1.call-update) | async-done | bytes 589840 | tf_op jit(solution)/shard_map/reduce_scatter | solution.py:63
  345.0 2.1 add_convert_fusion
  (35 shorter events, 0.5 us)
Async XLA Ops:
  6.5 232.7 %copy-start = (f32[16,6144]{1,0:T(8,128)S(1)}, f32[16,6144]{1,0:T(8,128)}, u32[]{:S(2)}) copy-start(f32[16,6144]{1,0:T(8,128)} %param.13) | copy-start | bytes 1179652
  6.5 10.6 %copy-start.5 = (s32[16,2]{0,1:T(2,128)S(1)}, s32[16,2]{0,1:T(2,128)}, u32[]{:S(2)}) copy-start(s32[16,2]{0,1:T(2,128)} %param.15) | copy-start | bytes 388
  6.5 186.6 %all-reduce.2.cloned.1.call-start = ((), (), s32[]{:S(2)}) async-start(), calls=%async_computation.1 | async-start | bytes 2359296 | tf_op jit(solution)/shard_map/psum | solution.py:12
  11.5 183.0 %copy-start.1 = (bf16[768,384]{1,0:T(8,128)(2,1)S(1)}, bf16[768,384]{1,0:T(8,128)(2,1)}, u32[]{:S(2)}) copy-start(bf16[768,384]{1,0:T(8,128)(2,1)} %param.10) | copy-start | bytes 1769476
  11.5 36.9 %collective-permute-start = (bf16[2,768,384]{2,1,0:T(8,128)(2,1)}, bf16[2,768,384]{2,1,0:T(8,128)(2,1)S(1)}, u32[]{:S(2)}, u32[]{:S(2)}) collective-permute-start(bf16[2,768,384]{2,1,0:T(8,128)(2,1)} %get-tuple-element.17), channel_id=1, source_target_pairs={{0,16},{16,32},{32,48},{48,64},{64,80},{80,96},{96,112},{112,128},... | collective-permute-start | bytes 3538952 | tf_op jit(solution)/shard_map/ppermute | solution.py:18
  14.5 34.0 %collective-permute-start.1 = (bf16[2,768,384]{2,1,0:T(8,128)(2,1)}, bf16[2,768,384]{2,1,0:T(8,128)(2,1)}, u32[]{:S(2)}, u32[]{:S(2)}) collective-permute-start(bf16[2,768,384]{2,1,0:T(8,128)(2,1)} %get-tuple-element.17), channel_id=1, source_target_pairs={{0,32},{16,48},{32,64},{48,80},{64,96},{80,112},{96,128},{112,144}... | collective-permute-start | bytes 3538952 | tf_op jit(solution)/shard_map/ppermute | solution.py:18
  16.4 328.6 %reduce-scatter.2.cloned.1.call-start = ((), (), s32[]{:S(2)}) async-start(), calls=%async_computation.2 | async-start | bytes 10027008 | tf_op jit(solution)/shard_map/reduce_scatter | solution.py:63
  194.5 10.7 %copy-start.4 = (bf16[768,384]{1,0:T(8,128)(2,1)S(1)}, bf16[768,384]{1,0:T(8,128)(2,1)}, u32[]{:S(2)}) copy-start(bf16[768,384]{1,0:T(8,128)(2,1)} %param.8) | copy-start | bytes 1769476
  208.1 8.3 %copy-start.2 = (bf16[3072,384]{1,0:T(8,128)(2,1)S(1)}, bf16[3072,384]{1,0:T(8,128)(2,1)}, u32[]{:S(2)}) copy-start(bf16[3072,384]{1,0:T(8,128)(2,1)} %get-tuple-element.24) | copy-start | bytes 7077892
  216.5 3.1 slice-start
  216.5 3.5 slice-start.1
  216.5 3.7 %slice-start.2 = ((s8[9437184]{0:T(1024)(128)(4,1)}), s8[1048576]{0:T(1024)(128)(4,1)S(1)}, s32[]{:S(2)}) async-start(s8[9437184]{0:T(1024)(128)(4,1)} %bitcast.23), calls=%async_computation.5 | async-start | bytes 2097152
  224.2 6.2 %slice-start.3 = ((s8[4718592]{0:T(1024)(128)(4,1)}), s8[524288]{0:T(1024)(128)(4,1)S(1)}, s32[]{:S(2)}) async-start(s8[4718592]{0:T(1024)(128)(4,1)} %bitcast.28), calls=%async_computation.6 | async-start | bytes 1048576
  227.3 3.1 slice-start.4
  237.9 0.7 copy-start.6
  237.9 107.1 %copy-start.3 = (bf16[48,6144]{1,0:T(8,128)(2,1)S(1)}, bf16[48,6144]{1,0:T(8,128)(2,1)}, u32[]{:S(2)}) copy-start(bf16[48,6144]{1,0:T(8,128)(2,1)} %param.11) | copy-start | bytes 1769476
Sparse Core Ops, SparseCore 0:
  16.6 176.4 all-reduce.1
  238.1 106.8 reduce-scatter.1
where the time goes:
time: 356 us; the launch traced here: 354 us
  waiting for transfers between devices  277 us (78%)
  matrix products  29 us (8%)
  other arithmetic  21 us (6%)
  between operations  16.2 us (5%)
  local copies, waits for them, and re-layouts  5.35 us (2%)
  starting transfers between devices  4.99 us (1%)
    psum x1, waiting for transfers between devices, spread(): return lax.psum(kept, axis)  143 us
    reduce_scatter x1, waiting for transfers between devices, local(): lax.psum_scatter(head_terms.astype(jnp.bfloat16), 'mp', scatter_dimension...  105 us
    ppermute x2, waiting for transfers between devices, from_behind(): return lax.ppermute(value, axis, pairs)  29.2 us
    dot_general x3, matrix products, attend_head(): jnp.dot(query_rows, key_rows.T, preferred_element_type=jnp.float32)  11.3 us
    concatenate x1, other arithmetic, local(): all_keys = jnp.concatenate(key_parts, 0)  10.6 us
    dot_general x3, matrix products, attend_head(): jnp.dot(weights_bf, value_rows, preferred_element_type=jnp.float32)  9.24 us
    dot_general x1, matrix products, local(): jnp.dot(attended, out_weight, preferred_element_type=jnp.float32)  7.56 us
  transfers between devices with their start and end apart: 4, of which 3 were waited for; matrix products, arithmetic and copies ran while one was open for 1% of the time, Pallas kernels for 0%

commit v1 on v0

v1 whole, which is shorter than its diff:
```python
import math

import jax
import jax.numpy as jnp
from jax import lax
from jax.experimental import pallas as pl
from jax.experimental.pallas import tpu as pltpu
from jax.sharding import Mesh, PartitionSpec as P

HD = 128
HEADS_HERE = 3
NZ, NXH, NY, NXL, NC = 8, 2, 4, 2, 2
X_FIRST = 2688
LOG2E = math.log2(math.e)
SWAP = [(0, 1), (1, 0)]


def shift(value, axis, count, steps):
    return lax.ppermute(value, axis, [(i, (i + steps) % count) for i in range(count)])


def attend_body(scalar_ref, q_ref, k0, v0, k1, v1, k2, v2, *rest):
    pieces, (out_ref, peak_ref, total_ref, k3, v3) = rest[:NZ], rest[NZ:]
    factor = HD ** (-0.5) * LOG2E
    share = q_ref.shape[1]
    rows = k0.shape[0]
    piece_rows = rows // NZ
    y, xl, core = scalar_ref[4], scalar_ref[5], scalar_ref[6]
    step = pl.program_id(0)
    blocks = ((k0, v0), (k1, v1), (k2, v2), (k3, v3))
    ones = jnp.ones((rows, HD), jnp.bfloat16)

    @pl.when(step == 0)
    def _():
        for number, piece in enumerate(pieces):
            k3[pl.ds(number * piece_rows, piece_rows)] = piece[0]
            v3[pl.ds(number * piece_rows, piece_rows)] = piece[1]

    places = []
    for xl_step in range(NXL):
        for y_step in range(NY):
            y_there = lax.rem(y + y_step, NY)
            xl_there = lax.rem(xl + xl_step, NXL)
            places.append((y_there * NXL + xl_there) * NC + lax.rem(core + step, NC))

    def queries_of(head):
        return jnp.concatenate([q_ref[place, :, head * HD : (head + 1) * HD] for place in places], axis=0)

    for number, (k_ref, v_ref) in enumerate(blocks):

        def one_block(number=number, k_ref=k_ref, v_ref=v_ref):
            for head in range(HEADS_HERE):
                cols = slice(head * HD, (head + 1) * HD)
                scores = lax.dot_general(
                    queries_of(head), k_ref[:, cols], (((1,), (1,)), ((), ())), preferred_element_type=jnp.float32
                )
                block_peak = jnp.max(scores, axis=1, keepdims=True)
                if number == 0:
                    peak = block_peak
                else:
                    old_peak = peak_ref[head]
                    peak = jnp.maximum(old_peak, block_peak)
                probs = jnp.exp2((scores - peak) * factor).astype(jnp.bfloat16)
                wide = jnp.concatenate([v_ref[:, cols], ones], axis=1)
                added = jnp.dot(probs, wide, preferred_element_type=jnp.float32)
                if number == 0:
                    total_ref[head] = added
                else:
                    total_ref[head] = total_ref[head] * jnp.exp2((old_peak - peak) * factor) + added
                peak_ref[head] = peak

        if number == 0:
            one_block()
        else:
            pl.when(scalar_ref[number] == 1)(one_block)
    for head in range(HEADS_HERE):
        total = total_ref[head]
        out_ref[:, head * HD : (head + 1) * HD] = (total[:, :HD] / total[:, HD:]).astype(jnp.bfloat16)


def attend(scalars, queries, blocks, pieces):
    rows, width = queries.shape
    share = rows // (NY * NXL * NC)
    tile = rows // NC
    whole = pl.BlockSpec((rows, width), lambda i, *_: (0, 0))
    return pl.pallas_call(
        attend_body,
        out_shape=jax.ShapeDtypeStruct((rows, width), jnp.bfloat16),
        grid_spec=pltpu.PrefetchScalarGridSpec(
            num_scalar_prefetch=1,
            grid=(NC,),
            in_specs=[pl.BlockSpec((NY * NXL * NC, share, width), lambda i, *_: (0, 0, 0))]
            + [whole] * len(blocks)
            + [pl.BlockSpec((2, rows // NZ, width), lambda i, *_: (0, 0, 0))] * len(pieces),
            out_specs=pl.BlockSpec((tile, width), lambda i, *_: (i, 0)),
            scratch_shapes=[
                pltpu.VMEM((HEADS_HERE, tile, 1), jnp.float32),
                pltpu.VMEM((HEADS_HERE, tile, 2 * HD), jnp.float32),
                pltpu.VMEM((rows, width), jnp.bfloat16),
                pltpu.VMEM((rows, width), jnp.bfloat16),
            ],
        ),
        compiler_params=pltpu.CompilerParams(vmem_limit_bytes=40 * 1024 * 1024),
        cost_estimate=pl.CostEstimate(
            flops=16 * rows * rows * width, bytes_accessed=20 * rows * width, transcendentals=12 * rows * rows
        ),
    )(scalars, queries.reshape(NY * NXL * NC, share, width), *blocks, *pieces)


def spread_clean(keys, values, root, z, xh):
    rows, width = keys.shape
    own = jnp.stack([keys.reshape(NZ, rows // NZ, width), values.reshape(NZ, rows // NZ, width)], axis=1)
    distance = lax.rem(z - root // NXH + NZ, NZ)
    at_root = distance == 0
    up, down = own[4], own[5]
    for number in range(4):
        up = shift(jnp.where(at_root, own[4 - number], up) if number else up, "z", NZ, 1)
        if number < 3:
            down = shift(jnp.where(at_root, own[5 + number], down) if number else down, "z", NZ, -1)
    piece = jnp.where(at_root, own[0], jnp.where(distance <= 4, up, down))
    piece = jnp.where(xh == lax.rem(root, NXH), piece, lax.ppermute(piece, "xh", SWAP))
    pieces = [piece]
    up = down = piece
    for number in range(4):
        up = shift(up, "z", NZ, 1)
        pieces.append(up)
        if number < 3:
            down = shift(down, "z", NZ, -1)
            pieces.append(down)
    return pieces


def add(*terms):
    total = terms[0].astype(jnp.float32)
    for term in terms[1:]:
        total = total + term.astype(jnp.float32)
    return total


def sum_over_y(terms):
    half = terms[0].shape[-1] // 2
    from_below = shift(terms[2][..., :half], "y", NY, 1)
    from_above = shift(terms[2][..., half:], "y", NY, -1)
    rise = jnp.concatenate([add(terms[1][..., :half], from_below).astype(jnp.bfloat16), terms[1][..., half:]], axis=-1)
    fall = jnp.concatenate([terms[3][..., :half], add(terms[3][..., half:], from_above).astype(jnp.bfloat16)], axis=-1)
    return [terms[0], shift(rise, "y", NY, 1), shift(fall, "y", NY, -1)]


def local(queries, keys, values, residual, out_weight, gate_table, noise_steps, windows):
    z, xh, y, xl, core = (lax.axis_index(name) for name in ("z", "xh", "y", "xl", "c"))
    my_span = z * NXH + xh
    span_ids = lax.iota(jnp.int32, NZ * NXH)
    clean_root = jnp.sum(span_ids * (noise_steps == 0).astype(jnp.int32))
    rows, width = queries.shape
    share = residual.shape[0]

    lag2_keys, lag2_values = shift(keys, "z", NZ, 1), shift(values, "z", NZ, 1)
    pieces = spread_clean(keys, values, clean_root, z, xh)
    lag1_keys = lax.ppermute(jnp.where(xh == 0, keys, lag2_keys), "xh", SWAP)
    lag1_values = lax.ppermute(jnp.where(xh == 0, values, lag2_values), "xh", SWAP)
    sibling_weight = lax.ppermute(out_weight, "c", SWAP)

    scalars = jnp.stack(
        [
            jnp.int32(1),
            windows[my_span, 1],
            windows[my_span, 0],
            (my_span != clean_root).astype(jnp.int32),
            y,
            xl,
            core,
        ]
    )
    blocks = [keys, values, lag2_keys, lag2_values, lag1_keys, lag1_values]
    attended = attend(scalars, queries, blocks, pieces)
    taken = lax.ppermute(attended[rows // 2 :], "c", SWAP)
    both = jnp.concatenate([attended[: rows // 2], taken], axis=1)
    weight = jnp.concatenate([out_weight, sibling_weight], axis=0)

    def project(low, high):
        terms = jnp.dot(both, weight[:, low:high], preferred_element_type=jnp.float32).astype(jnp.bfloat16)
        return terms.reshape(NXL, NY, share, high - low)

    x_first = project(0, X_FIRST)
    y_first = project(X_FIRST, out_weight.shape[1])

    x_got = lax.ppermute(x_first[1], "xl", SWAP)
    here = sum_over_y([y_first[:, number] for number in range(NY)])
    here_kept = [term[0] for term in here]
    here_sent = add(*[term[1] for term in here]).astype(jnp.bfloat16)
    here_got = lax.ppermute(here_sent, "xl", SWAP)
    x_sum = add(x_first[0], x_got).astype(jnp.bfloat16)
    left = add(*sum_over_y([x_sum[number] for number in range(NY)]))
    right = add(*here_kept, here_got)
    gate_row = lax.dynamic_slice_in_dim(gate_table, noise_steps[my_span], 1, 0)
    summed = jnp.concatenate([left, right], axis=1)
    return (residual.astype(jnp.float32) + gate_row * summed).astype(jnp.bfloat16)


def solution(mesh):
    fine = Mesh(mesh.devices.reshape(NZ, NXH, NY, NXL, NC), ("z", "xh", "y", "xl", "c"))
    span, mp = ("z", "xh"), ("y", "xl", "c")
    in_specs = (
        P(span, mp),
        P(span, mp),
        P(span, mp),
        P(span + mp, None),
        P(mp, None),
        P(),
        P(),
        P(),
    )
    out_specs = P(span + mp, None)
    return jax.shard_map(local, mesh=fine, in_specs=in_specs, out_specs=out_specs, check_vma=False)
```

time: 356 us -> 162 us (0.46)
  the two profiles are of different devices: /device:TPU:24 before, /device:TPU:68 now
where the time goes in v1:
time: 162 us; the launch traced here: 158 us
  waiting for transfers between devices  67.4 us (42%)
  starting transfers between devices  47.9 us (30%)
  local copies, waits for them, and re-layouts  13.7 us (8%)
  Pallas kernels  13.1 us (8%)
  other arithmetic  6.36 us (4%)
  between operations  5.76 us (4%)
  matrix products  4.13 us (3%)
    ppermute x24, waiting for transfers between devices, shift(): lax.ppermute(value, axis, [(i, (i + steps) % count) for i in range(count)])  40.9 us
    ppermute x24, starting transfers between devices, shift(): lax.ppermute(value, axis, [(i, (i + steps) % count) for i in range(count)])  38.1 us
    ppermute x1, waiting for transfers between devices, local(): x_got = lax.ppermute(x_first[1], 'xl', SWAP)  15.2 us
    pallas_call x1, Pallas kernels, attend(): pl.pallas_call(attend_body, out_shape=jax.ShapeDtypeStruct((rows, width),...  13.1 us
    unnamed x25, local copies, waits for them, and re-layouts  7.52 us
    ppermute x1, waiting for transfers between devices, local(): lax.ppermute(jnp.where(xh == 0, values, lag2_values), 'xh', SWAP)  6.32 us
    dot_general x2, matrix products, project(): jnp.dot(both, weight[:, low:high], preferred_element_type=jnp.float32)  4.13 us
  transfers between devices with their start and end apart: 31, of which 20 were waited for; matrix products, arithmetic and copies ran while one was open for 11% of the time, Pallas kernels for 8%

profile of v1, /device:TPU:68, one launch (start us, length us, event | category | flops | bytes accessed | tf_op | source)
XLA Modules:
  0.0 158.4 jit_solution(13729612624859902748)
XLA Ops:
  7.5 2.6 %collective-permute-start.5 = (bf16[2,96,384]{2,1,0:T(8,128)(2,1)S(1)}, bf16[2,96,384]{2,1,0:T(8,128)(2,1)S(1)}, u32[]{:S(2)}, u32[]{:S(2)}) collective-permute-start(bf16[2,96,384]{2,1,0:T(8,128)(2,1)S(1)} %bitcast_select_fusion.2), channel_id=1, source_target_pairs={{0,32},{32,64},{64,96},{96,128},{128,160},{160,192},{192,224},{224... | collective-permute-start | bytes 442376 | tf_op jit(solution)/shard_map/ppermute | solution.py:19
  10.5 2.9 %collective-permute-done.5 = bf16[2,96,384]{2,1,0:T(8,128)(2,1)S(1)} collective-permute-done((bf16[2,96,384]{2,1,0:T(8,128)(2,1)S(1)}, bf16[2,96,384]{2,1,0:T(8,128)(2,1)S(1)}, u32[]{:S(2)}, u32[]{:S(2)}) %collective-permute-start.5) | collective-permute-done | bytes 147488 | tf_op jit(solution)/shard_map/ppermute | solution.py:19
  13.5 2.4 %collective-permute-start.9 = (bf16[2,96,384]{2,1,0:T(8,128)(2,1)S(1)}, bf16[2,96,384]{2,1,0:T(8,128)(2,1)S(1)}, u32[]{:S(2)}, u32[]{:S(2)}) collective-permute-start(bf16[2,96,384]{2,1,0:T(8,128)(2,1)S(1)} %get-tuple-element.12), channel_id=1, source_target_pairs={{0,224},{32,0},{64,32},{96,64},{128,96},{160,128},{192,160},{224,1... | collective-permute-start | bytes 442376 | tf_op jit(solution)/shard_map/ppermute | solution.py:19
  17.0 3.0 %collective-permute-done.9 = bf16[2,96,384]{2,1,0:T(8,128)(2,1)S(1)} collective-permute-done((bf16[2,96,384]{2,1,0:T(8,128)(2,1)S(1)}, bf16[2,96,384]{2,1,0:T(8,128)(2,1)S(1)}, u32[]{:S(2)}, u32[]{:S(2)}) %collective-permute-start.9) | collective-permute-done | bytes 147488 | tf_op jit(solution)/shard_map/ppermute | solution.py:19
  24.2 3.0 %collective-permute-done.7 = bf16[2,96,384]{2,1,0:T(8,128)(2,1)S(1)} collective-permute-done((bf16[2,96,384]{2,1,0:T(8,128)(2,1)S(1)}, bf16[2,96,384]{2,1,0:T(8,128)(2,1)S(1)}, u32[]{:S(2)}, u32[]{:S(2)}) %collective-permute-start.7) | collective-permute-done | bytes 147488 | tf_op jit(solution)/shard_map/ppermute | solution.py:19
  27.2 3.1 %collective-permute-done.10 = bf16[2,96,384]{2,1,0:T(8,128)(2,1)S(1)} collective-permute-done((bf16[2,96,384]{2,1,0:T(8,128)(2,1)S(1)}, bf16[2,96,384]{2,1,0:T(8,128)(2,1)S(1)}, u32[]{:S(2)}, u32[]{:S(2)}) %collective-permute-start.10) | collective-permute-done | bytes 147488 | tf_op jit(solution)/shard_map/ppermute | solution.py:19
  30.9 3.2 %collective-permute-start = (bf16[768,384]{1,0:T(8,128)(2,1)S(1)}, bf16[768,384]{1,0:T(8,128)(2,1)S(1)}, u32[]{:S(2)}, u32[]{:S(2)}) collective-permute-start(bf16[768,384]{1,0:T(8,128)(2,1)S(1)} %copy-done.1), channel_id=1, source_target_pairs={{0,32},{32,64},{64,96},{96,128},{128,160},{160,192},{192,224},{224... | collective-permute-start | bytes 1769480 | tf_op jit(solution)/shard_map/ppermute | solution.py:19
  34.2 2.9 %collective-permute-done.11 = bf16[2,96,384]{2,1,0:T(8,128)(2,1)S(1)} collective-permute-done((bf16[2,96,384]{2,1,0:T(8,128)(2,1)S(1)}, bf16[2,96,384]{2,1,0:T(8,128)(2,1)S(1)}, u32[]{:S(2)}, u32[]{:S(2)}) %collective-permute-start.11) | collective-permute-done | bytes 147488 | tf_op jit(solution)/shard_map/ppermute | solution.py:121
  37.1 3.3 %collective-permute-start.12 = (bf16[2,96,384]{2,1,0:T(8,128)(2,1)S(1)}, bf16[2,96,384]{2,1,0:T(8,128)(2,1)}, u32[]{:S(2)}, u32[]{:S(2)}) collective-permute-start(bf16[2,96,384]{2,1,0:T(8,128)(2,1)S(1)} %broadcast_select_fusion.2.rest_0_), channel_id=1, source_target_pairs={{0,32},{32,64},{64,96},{96,128},{128,160},{160,192},{192,224},{224... | collective-permute-start | bytes 442376 | tf_op jit(solution)/shard_map/ppermute | solution.py:19
  40.4 5.0 %constant_dynamic-update-slice_fusion.1 = bf16[768,6144]{1,0:T(8,128)(2,1)} fusion(bf16[384,6144]{1,0:T(8,128)(2,1)} %param.12), kind=kLoop, calls=%fused_computation.73 | loop fusion | bytes 9437184
  48.1 12.1 %collective-permute-done.12.rest_1_ = bf16[2,96,384]{2,1,0:T(8,128)(2,1)} collective-permute-done((bf16[2,96,384]{2,1,0:T(8,128)(2,1)S(1)}, bf16[2,96,384]{2,1,0:T(8,128)(2,1)}, u32[]{:S(2)}, u32[]{:S(2)}) %collective-permute-start.12) | collective-permute-done | bytes 147488 | tf_op jit(solution)/shard_map/ppermute | solution.py:19
  60.2 2.6 %collective-permute-start.14 = (bf16[2,96,384]{2,1,0:T(8,128)(2,1)}, bf16[2,96,384]{2,1,0:T(8,128)(2,1)S(1)}, u32[]{:S(2)}, u32[]{:S(2)}) collective-permute-start(bf16[2,96,384]{2,1,0:T(8,128)(2,1)} %collective-permute-done.12.rest_1_), channel_id=1, source_target_pairs={{0,32},{32,64},{64,96},{96,128},{128,160},{160,192},{192,224},{224... | collective-permute-start | bytes 442376 | tf_op jit(solution)/shard_map/ppermute | solution.py:19
  63.7 3.0 %collective-permute-start.2 = (bf16[768,384]{1,0:T(8,128)(2,1)}, bf16[768,384]{1,0:T(8,128)(2,1)}, u32[]{:S(2)}, u32[]{:S(2)}) collective-permute-start(bf16[768,384]{1,0:T(8,128)(2,1)} %broadcast_select_fusion.1), channel_id=1, source_target_pairs={{0,16},{16,0},{1,17},{17,1},{2,18},{18,2},{3,19},{19,3},{4,20},{20... | collective-permute-start | bytes 1769480 | tf_op jit(solution)/shard_map/ppermute | solution.py:159
  72.6 2.5 %collective-permute-start.18 = (bf16[2,96,384]{2,1,0:T(8,128)(2,1)}, bf16[2,96,384]{2,1,0:T(8,128)(2,1)}, u32[]{:S(2)}, u32[]{:S(2)}) collective-permute-start(bf16[2,96,384]{2,1,0:T(8,128)(2,1)} %collective-permute-done.16.rest_5_), channel_id=1, source_target_pairs={{0,32},{32,64},{64,96},{96,128},{128,160},{160,192},{192,224},{224... | collective-permute-start | bytes 442376 | tf_op jit(solution)/shard_map/ppermute | solution.py:19
  80.0 6.3 %collective-permute-done.3.v2 = bf16[768,384]{1,0:T(8,128)(2,1)} collective-permute-done((bf16[768,384]{1,0:T(8,128)(2,1)}, bf16[768,384]{1,0:T(8,128)(2,1)}, u32[]{:S(2)}, u32[]{:S(2)}) %collective-permute-start.3) | collective-permute-done | bytes 589856 | tf_op jit(solution)/shard_map/ppermute | solution.py:160
  88.2 13.1 %shard_map.82 = bf16[768,384]{1,0:T(8,128)(2,1)S(1)} custom-call(s32[7]{0:T(128)S(1)} %stack.26.scalar_ref, bf16[16,48,384]{2,1,0:T(8,128)(2,1)S(1)} %bitcast.92, bf16[768,384]{1,0:T(8,128)(2,1)S(1)} %copy-done.1, bf16[768,384]{1,0:T(8,128)(2,1)S(1)} %copy-done.2, bf16[768,384]{1,0:T(8,128)(2,1)S(1)} %collective-permute-done.k1, ...), custom_call_target="tpu_custom_call" | custom-call | flops 3623878656 | bytes 5898240 | tf_op jit(solution)/shard_map/pallas_call | solution.py:86
  101.7 2.6 %constant_dynamic-update-slice_fusion = bf16[768,6144]{1,0:T(8,128)(2,1)S(1)} fusion(bf16[768,6144]{1,0:T(8,128)(2,1)S(1)} %copy-done.8, bf16[384,6144]{1,0:T(8,128)(2,1)} %collective-permute-done.20), kind=kLoop, calls=%fused_computation.72 | loop fusion | bytes 9437184 | tf_op jit(solution)/shard_map/concatenate | solution.py:178
  107.0 3.1 %collective-permute-start.28 = (bf16[2,48,1728]{2,1,0:T(8,128)(2,1)S(1)}, bf16[2,48,1728]{2,1,0:T(8,128)(2,1)S(1)}, u32[]{:S(2)}, u32[]{:S(2)}) collective-permute-start(bf16[2,48,1728]{2,1,0:T(8,128)(2,1)S(1)} %get-tuple-element.20), channel_id=1, source_target_pairs={{0,12},{4,0},{8,4},{12,8},{1,13},{5,1},{9,5},{13,9},{2,14},{6,2},{... | collective-permute-start | bytes 995336 | tf_op jit(solution)/shard_map/ppermute | solution.py:19
  114.5 3.5 %collective-permute-done.28 = bf16[2,48,1728]{2,1,0:T(8,128)(2,1)S(1)} collective-permute-done((bf16[2,48,1728]{2,1,0:T(8,128)(2,1)S(1)}, bf16[2,48,1728]{2,1,0:T(8,128)(2,1)S(1)}, u32[]{:S(2)}, u32[]{:S(2)}) %collective-permute-start.28) | collective-permute-done | bytes 331808 | tf_op jit(solution)/shard_map/ppermute | solution.py:19
  118.3 3.8 %collective-permute-start.29 = (bf16[2,48,3456]{2,1,0:T(8,128)(2,1)S(1)}, bf16[2,48,3456]{2,1,0:T(8,128)(2,1)S(1)}, u32[]{:S(2)}, u32[]{:S(2)}) collective-permute-start(bf16[2,48,3456]{2,1,0:T(8,128)(2,1)S(1)} %pad_maximum_fusion.1), channel_id=1, source_target_pairs={{0,12},{4,0},{8,4},{12,8},{1,13},{5,1},{9,5},{13,9},{2,14},{6,2},{... | collective-permute-start | bytes 1990664 | tf_op jit(solution)/shard_map/ppermute | solution.py:19
  122.5 15.2 %collective-permute-done.21 = bf16[4,48,2688]{2,1,0:T(8,128)(2,1)S(1)} collective-permute-done((bf16[4,48,2688]{2,1,0:T(8,128)(2,1)S(1)}, bf16[4,48,2688]{2,1,0:T(8,128)(2,1)S(1)}, u32[]{:S(2)}, u32[]{:S(2)}) %collective-permute-start.21) | collective-permute-done | bytes 1032224 | tf_op jit(solution)/shard_map/ppermute | solution.py:187
  138.1 3.0 %collective-permute-start.24 = (bf16[48,1344]{1,0:T(8,128)(2,1)S(1)}, bf16[48,1344]{1,0:T(8,128)(2,1)S(1)}, u32[]{:S(2)}, u32[]{:S(2)}) collective-permute-start(bf16[48,1344]{1,0:T(8,128)(2,1)S(1)} %get-tuple-element.24), channel_id=1, source_target_pairs={{0,12},{4,0},{8,4},{12,8},{1,13},{5,1},{9,5},{13,9},{2,14},{6,2},{... | collective-permute-start | bytes 387080 | tf_op jit(solution)/shard_map/ppermute | solution.py:19
  143.9 3.7 %collective-permute-start.25 = (bf16[48,2688]{1,0:T(8,128)(2,1)S(1)}, bf16[48,2688]{1,0:T(8,128)(2,1)S(1)}, u32[]{:S(2)}, u32[]{:S(2)}) collective-permute-start(bf16[48,2688]{1,0:T(8,128)(2,1)S(1)} %pad_maximum_fusion.6), channel_id=1, source_target_pairs={{0,12},{4,0},{8,4},{12,8},{1,13},{5,1},{9,5},{13,9},{2,14},{6,2},{... | collective-permute-start | bytes 774152 | tf_op jit(solution)/shard_map/ppermute | solution.py:19
  151.5 5.8 %collective-permute-done.23 = bf16[48,2688]{1,0:T(8,128)(2,1)S(1)} collective-permute-done((bf16[48,2688]{1,0:T(8,128)(2,1)S(1)}, bf16[48,2688]{1,0:T(8,128)(2,1)S(1)}, u32[]{:S(2)}, u32[]{:S(2)}) %collective-permute-start.23) | collective-permute-done | bytes 258080 | tf_op jit(solution)/shard_map/ppermute | solution.py:19
  (103 shorter events, 40.8 us)
Async XLA Ops:
  0.0 101.6 %collective-permute-start.20 = (bf16[384,6144]{1,0:T(8,128)(2,1)}, bf16[384,6144]{1,0:T(8,128)(2,1)}, u32[]{:S(2)}, u32[]{:S(2)}) collective-permute-start(bf16[384,6144]{1,0:T(8,128)(2,1)} %param.12), channel_id=1, source_target_pairs={{0,1},{1,0},{2,3},{3,2},{4,5},{5,4},{6,7},{7,6},{8,9},{9,8},{10,11... | collective-permute-start | bytes 14155784 | tf_op jit(solution)/shard_map/ppermute | solution.py:161
  1.3 6.3 %collective-permute-start.4 = (bf16[2,96,384]{2,1,0:T(8,128)(2,1)S(1)}, bf16[2,96,384]{2,1,0:T(8,128)(2,1)S(1)}, u32[]{:S(2)}, u32[]{:S(2)}) collective-permute-start(bf16[2,96,384]{2,1,0:T(8,128)(2,1)S(1)} %get-tuple-element.15), channel_id=1, source_target_pairs={{0,32},{32,64},{64,96},{96,128},{128,160},{160,192},{192,224},{224... | collective-permute-start | bytes 442376 | tf_op jit(solution)/shard_map/ppermute | solution.py:19
  3.2 7.3 %collective-permute-start.8 = (bf16[2,96,384]{2,1,0:T(8,128)(2,1)S(1)}, bf16[2,96,384]{2,1,0:T(8,128)(2,1)S(1)}, u32[]{:S(2)}, u32[]{:S(2)}) collective-permute-start(bf16[2,96,384]{2,1,0:T(8,128)(2,1)S(1)} %get-tuple-element.14), channel_id=1, source_target_pairs={{0,224},{32,0},{64,32},{96,64},{128,96},{160,128},{192,160},{224,1... | collective-permute-start | bytes 442376 | tf_op jit(solution)/shard_map/ppermute | solution.py:19
  13.5 6.6 %collective-permute-start.9 = (bf16[2,96,384]{2,1,0:T(8,128)(2,1)S(1)}, bf16[2,96,384]{2,1,0:T(8,128)(2,1)S(1)}, u32[]{:S(2)}, u32[]{:S(2)}) collective-permute-start(bf16[2,96,384]{2,1,0:T(8,128)(2,1)S(1)} %get-tuple-element.12), channel_id=1, source_target_pairs={{0,224},{32,0},{64,32},{96,64},{128,96},{160,128},{192,160},{224,1... | collective-permute-start | bytes 442376 | tf_op jit(solution)/shard_map/ppermute | solution.py:19
  23.9 6.4 %collective-permute-start.10 = (bf16[2,96,384]{2,1,0:T(8,128)(2,1)S(1)}, bf16[2,96,384]{2,1,0:T(8,128)(2,1)S(1)}, u32[]{:S(2)}, u32[]{:S(2)}) collective-permute-start(bf16[2,96,384]{2,1,0:T(8,128)(2,1)S(1)} %get-tuple-element.10), channel_id=1, source_target_pairs={{0,224},{32,0},{64,32},{96,64},{128,96},{160,128},{192,160},{224,1... | collective-permute-start | bytes 442376 | tf_op jit(solution)/shard_map/ppermute | solution.py:19
  30.3 6.7 %collective-permute-start.11 = (bf16[2,96,384]{2,1,0:T(8,128)(2,1)S(1)}, bf16[2,96,384]{2,1,0:T(8,128)(2,1)S(1)}, u32[]{:S(2)}, u32[]{:S(2)}) collective-permute-start(bf16[2,96,384]{2,1,0:T(8,128)(2,1)S(1)} %bitcast_select_fusion.5), channel_id=1, source_target_pairs={{0,16},{16,0},{1,17},{17,1},{2,18},{18,2},{3,19},{19,3},{4,20},{20... | collective-permute-start | bytes 442376 | tf_op jit(solution)/shard_map/ppermute | solution.py:121
  30.9 31.8 %collective-permute-start = (bf16[768,384]{1,0:T(8,128)(2,1)S(1)}, bf16[768,384]{1,0:T(8,128)(2,1)S(1)}, u32[]{:S(2)}, u32[]{:S(2)}) collective-permute-start(bf16[768,384]{1,0:T(8,128)(2,1)S(1)} %copy-done.1), channel_id=1, source_target_pairs={{0,32},{32,64},{64,96},{96,128},{128,160},{160,192},{192,224},{224... | collective-permute-start | bytes 1769480 | tf_op jit(solution)/shard_map/ppermute | solution.py:19
  34.2 35.2 %collective-permute-start.1 = (bf16[768,384]{1,0:T(8,128)(2,1)S(1)}, bf16[768,384]{1,0:T(8,128)(2,1)S(1)}, u32[]{:S(2)}, u32[]{:S(2)}) collective-permute-start(bf16[768,384]{1,0:T(8,128)(2,1)S(1)} %copy-done.2), channel_id=1, source_target_pairs={{0,32},{32,64},{64,96},{96,128},{128,160},{160,192},{192,224},{224... | collective-permute-start | bytes 1769480 | tf_op jit(solution)/shard_map/ppermute | solution.py:19
  37.1 23.1 %collective-permute-start.12 = (bf16[2,96,384]{2,1,0:T(8,128)(2,1)S(1)}, bf16[2,96,384]{2,1,0:T(8,128)(2,1)}, u32[]{:S(2)}, u32[]{:S(2)}) collective-permute-start(bf16[2,96,384]{2,1,0:T(8,128)(2,1)S(1)} %broadcast_select_fusion.2.rest_0_), channel_id=1, source_target_pairs={{0,32},{32,64},{64,96},{96,128},{128,160},{160,192},{192,224},{224... | collective-permute-start | bytes 442376 | tf_op jit(solution)/shard_map/ppermute | solution.py:19
  48.0 18.7 %collective-permute-start.13 = (bf16[2,96,384]{2,1,0:T(8,128)(2,1)S(1)}, bf16[2,96,384]{2,1,0:T(8,128)(2,1)S(1)}, u32[]{:S(2)}, u32[]{:S(2)}) collective-permute-start(bf16[2,96,384]{2,1,0:T(8,128)(2,1)S(1)} %broadcast_select_fusion.2.rest_0_), channel_id=1, source_target_pairs={{0,224},{32,0},{64,32},{96,64},{128,96},{160,128},{192,160},{224,1... | collective-permute-start | bytes 442376 | tf_op jit(solution)/shard_map/ppermute | solution.py:19
  60.2 7.2 %collective-permute-start.14 = (bf16[2,96,384]{2,1,0:T(8,128)(2,1)}, bf16[2,96,384]{2,1,0:T(8,128)(2,1)S(1)}, u32[]{:S(2)}, u32[]{:S(2)}) collective-permute-start(bf16[2,96,384]{2,1,0:T(8,128)(2,1)} %collective-permute-done.12.rest_1_), channel_id=1, source_target_pairs={{0,32},{32,64},{64,96},{96,128},{128,160},{160,192},{192,224},{224... | collective-permute-start | bytes 442376 | tf_op jit(solution)/shard_map/ppermute | solution.py:19
  63.7 16.4 %collective-permute-start.2 = (bf16[768,384]{1,0:T(8,128)(2,1)}, bf16[768,384]{1,0:T(8,128)(2,1)}, u32[]{:S(2)}, u32[]{:S(2)}) collective-permute-start(bf16[768,384]{1,0:T(8,128)(2,1)} %broadcast_select_fusion.1), channel_id=1, source_target_pairs={{0,16},{16,0},{1,17},{17,1},{2,18},{18,2},{3,19},{19,3},{4,20},{20... | collective-permute-start | bytes 1769480 | tf_op jit(solution)/shard_map/ppermute | solution.py:159
  70.3 16.1 %collective-permute-start.3 = (bf16[768,384]{1,0:T(8,128)(2,1)}, bf16[768,384]{1,0:T(8,128)(2,1)}, u32[]{:S(2)}, u32[]{:S(2)}) collective-permute-start(bf16[768,384]{1,0:T(8,128)(2,1)} %broadcast_select_fusion), channel_id=1, source_target_pairs={{0,16},{16,0},{1,17},{17,1},{2,18},{18,2},{3,19},{19,3},{4,20},{20... | collective-permute-start | bytes 1769480 | tf_op jit(solution)/shard_map/ppermute | solution.py:160
  72.1 6.3 %collective-permute-start.17 = (bf16[2,96,384]{2,1,0:T(8,128)(2,1)}, bf16[2,96,384]{2,1,0:T(8,128)(2,1)}, u32[]{:S(2)}, u32[]{:S(2)}) collective-permute-start(bf16[2,96,384]{2,1,0:T(8,128)(2,1)} %collective-permute-done.15.rest_4_), channel_id=1, source_target_pairs={{0,224},{32,0},{64,32},{96,64},{128,96},{160,128},{192,160},{224,1... | collective-permute-start | bytes 442376 | tf_op jit(solution)/shard_map/ppermute | solution.py:19
  72.6 13.8 %collective-permute-start.18 = (bf16[2,96,384]{2,1,0:T(8,128)(2,1)}, bf16[2,96,384]{2,1,0:T(8,128)(2,1)}, u32[]{:S(2)}, u32[]{:S(2)}) collective-permute-start(bf16[2,96,384]{2,1,0:T(8,128)(2,1)} %collective-permute-done.16.rest_5_), channel_id=1, source_target_pairs={{0,32},{32,64},{64,96},{96,128},{128,160},{160,192},{192,224},{224... | collective-permute-start | bytes 442376 | tf_op jit(solution)/shard_map/ppermute | solution.py:19
  107.0 11.1 %collective-permute-start.28 = (bf16[2,48,1728]{2,1,0:T(8,128)(2,1)S(1)}, bf16[2,48,1728]{2,1,0:T(8,128)(2,1)S(1)}, u32[]{:S(2)}, u32[]{:S(2)}) collective-permute-start(bf16[2,48,1728]{2,1,0:T(8,128)(2,1)S(1)} %get-tuple-element.20), channel_id=1, source_target_pairs={{0,12},{4,0},{8,4},{12,8},{1,13},{5,1},{9,5},{13,9},{2,14},{6,2},{... | collective-permute-start | bytes 995336 | tf_op jit(solution)/shard_map/ppermute | solution.py:19
  110.2 11.9 %collective-permute-start.26 = (bf16[2,48,1728]{2,1,0:T(8,128)(2,1)S(1)}, bf16[2,48,1728]{2,1,0:T(8,128)(2,1)S(1)}, u32[]{:S(2)}, u32[]{:S(2)}) collective-permute-start(bf16[2,48,1728]{2,1,0:T(8,128)(2,1)S(1)} %get-tuple-element.19), channel_id=1, source_target_pairs={{0,4},{4,8},{8,12},{12,0},{1,5},{5,9},{9,13},{13,1},{2,6},{6,10},{... | collective-permute-start | bytes 995336 | tf_op jit(solution)/shard_map/ppermute | solution.py:19
  112.3 25.4 %collective-permute-start.21 = (bf16[4,48,2688]{2,1,0:T(8,128)(2,1)S(1)}, bf16[4,48,2688]{2,1,0:T(8,128)(2,1)S(1)}, u32[]{:S(2)}, u32[]{:S(2)}) collective-permute-start(bf16[4,48,2688]{2,1,0:T(8,128)(2,1)S(1)} %bitcast.97), channel_id=1, source_target_pairs={{0,2},{2,0},{1,3},{3,1},{4,6},{6,4},{5,7},{7,5},{8,10},{10,8},{9,1... | collective-permute-start | bytes 3096584 | tf_op jit(solution)/shard_map/ppermute | solution.py:187
  118.3 22.8 %collective-permute-start.29 = (bf16[2,48,3456]{2,1,0:T(8,128)(2,1)S(1)}, bf16[2,48,3456]{2,1,0:T(8,128)(2,1)S(1)}, u32[]{:S(2)}, u32[]{:S(2)}) collective-permute-start(bf16[2,48,3456]{2,1,0:T(8,128)(2,1)S(1)} %pad_maximum_fusion.1), channel_id=1, source_target_pairs={{0,12},{4,0},{8,4},{12,8},{1,13},{5,1},{9,5},{13,9},{2,14},{6,2},{... | collective-permute-start | bytes 1990664 | tf_op jit(solution)/shard_map/ppermute | solution.py:19
  122.4 18.8 %collective-permute-start.27 = (bf16[2,48,3456]{2,1,0:T(8,128)(2,1)S(1)}, bf16[2,48,3456]{2,1,0:T(8,128)(2,1)S(1)}, u32[]{:S(2)}, u32[]{:S(2)}) collective-permute-start(bf16[2,48,3456]{2,1,0:T(8,128)(2,1)S(1)} %pad_maximum_fusion), channel_id=1, source_target_pairs={{0,4},{4,8},{8,12},{12,0},{1,5},{5,9},{9,13},{13,1},{2,6},{6,10},{... | collective-permute-start | bytes 1990664 | tf_op jit(solution)/shard_map/ppermute | solution.py:19
  141.3 8.9 %collective-permute-start.30 = (bf16[48,3456]{1,0:T(8,128)(2,1)S(1)}, bf16[48,3456]{1,0:T(8,128)(2,1)S(1)}, u32[]{:S(2)}, u32[]{:S(2)}) collective-permute-start(bf16[48,3456]{1,0:T(8,128)(2,1)S(1)} %fusion.5), channel_id=1, source_target_pairs={{0,2},{2,0},{1,3},{3,1},{4,6},{6,4},{5,7},{7,5},{8,10},{10,8},{9,1... | collective-permute-start | bytes 995336 | tf_op jit(solution)/shard_map/ppermute | solution.py:191
  143.3 6.3 %collective-permute-start.22 = (bf16[48,1344]{1,0:T(8,128)(2,1)S(1)}, bf16[48,1344]{1,0:T(8,128)(2,1)S(1)}, u32[]{:S(2)}, u32[]{:S(2)}) collective-permute-start(bf16[48,1344]{1,0:T(8,128)(2,1)S(1)} %get-tuple-element.23), channel_id=1, source_target_pairs={{0,4},{4,8},{8,12},{12,0},{1,5},{5,9},{9,13},{13,1},{2,6},{6,10},{... | collective-permute-start | bytes 387080 | tf_op jit(solution)/shard_map/ppermute | solution.py:19
  143.9 7.6 %collective-permute-start.25 = (bf16[48,2688]{1,0:T(8,128)(2,1)S(1)}, bf16[48,2688]{1,0:T(8,128)(2,1)S(1)}, u32[]{:S(2)}, u32[]{:S(2)}) collective-permute-start(bf16[48,2688]{1,0:T(8,128)(2,1)S(1)} %pad_maximum_fusion.6), channel_id=1, source_target_pairs={{0,12},{4,0},{8,4},{12,8},{1,13},{5,1},{9,5},{13,9},{2,14},{6,2},{... | collective-permute-start | bytes 774152 | tf_op jit(solution)/shard_map/ppermute | solution.py:19
  149.7 7.6 %collective-permute-start.23 = (bf16[48,2688]{1,0:T(8,128)(2,1)S(1)}, bf16[48,2688]{1,0:T(8,128)(2,1)S(1)}, u32[]{:S(2)}, u32[]{:S(2)}) collective-permute-start(bf16[48,2688]{1,0:T(8,128)(2,1)S(1)} %pad_maximum_fusion.5), channel_id=1, source_target_pairs={{0,4},{4,8},{8,12},{12,0},{1,5},{5,9},{9,13},{13,1},{2,6},{6,10},{... | collective-permute-start | bytes 774152 | tf_op jit(solution)/shard_map/ppermute | solution.py:19
  (19 other events, 193.0 us)

commit v2 on v1

v2 whole, which is shorter than its diff:
```python
import functools
import math

import jax
import jax.numpy as jnp
from jax import lax
from jax.experimental import pallas as pl
from jax.experimental.pallas import tpu as pltpu
from jax.sharding import Mesh, PartitionSpec as P

HD = 128
HEADS_HERE = 3
NZ, NXH, NY, NXL, NC = 8, 2, 4, 2, 2
X_FIRST = 2688
CHUNK = 16
LOG2E = math.log2(math.e)
SWAP = [(0, 1), (1, 0)]


def shift(value, axis, count, steps):
    return lax.ppermute(value, axis, [(i, (i + steps) % count) for i in range(count)])


def attend_body(fresh, last, flags, *refs):
    refs = list(refs)
    scalar_ref, q_ref = refs.pop(0), refs.pop(0)
    scores_ref, probs_ref = refs.pop(), refs.pop()
    if last:
        clean = (refs.pop(), refs.pop())
        peak_ref, total_ref, out_ref = refs.pop(), refs.pop(), refs.pop()
    else:
        total_ref, peak_ref = refs.pop(), refs.pop()
    if not fresh:
        old_total_ref, old_peak_ref = refs.pop(), refs.pop()
        peak_ref[...] = old_peak_ref[...]
        total_ref[...] = old_total_ref[...]
    if last:
        pieces = refs
        piece_rows = pieces[0].shape[1]

        @pl.when(pl.program_id(0) == 0)
        def _():
            for number, piece in enumerate(pieces):
                for side in range(2):
                    clean[side][pl.ds(number * piece_rows, piece_rows)] = piece[side]

        blocks = [clean]
    else:
        blocks = list(zip(refs[::2], refs[1::2]))
    factor = HD ** (-0.5) * LOG2E
    tile = probs_ref.shape[1]
    ones = jnp.ones((blocks[0][0].shape[0], HD), jnp.bfloat16)
    y, xl, core = scalar_ref[4], scalar_ref[5], scalar_ref[6]
    places = []
    for xl_step in range(NXL):
        for y_step in range(NY):
            y_there = lax.rem(y + y_step, NY)
            xl_there = lax.rem(xl + xl_step, NXL)
            places.append((y_there * NXL + xl_there) * NC + lax.rem(core + pl.program_id(0), NC))

    def one_block(first, k_ref, v_ref):
        def take_scores(head):
            cols = slice(head * HD, (head + 1) * HD)
            rows = jnp.concatenate([q_ref[place, :, cols] for place in places], axis=0)
            scores_ref[head % 2] = lax.dot_general(
                rows, k_ref[:, cols], (((1,), (1,)), ((), ())), preferred_element_type=jnp.float32
            )

        take_scores(0)
        for head in range(HEADS_HERE):
            cols = slice(head * HD, (head + 1) * HD)
            if head + 1 < HEADS_HERE:
                take_scores(head + 1)
            scales = []
            for low in range(0, tile, CHUNK):
                rows = slice(low, low + CHUNK)
                scores = scores_ref[head % 2, rows]
                peak = jnp.max(scores, axis=1, keepdims=True)
                if not first:
                    old_peak = peak_ref[head, rows]
                    peak = jnp.maximum(old_peak, peak)
                    scales.append(jnp.exp2((old_peak - peak) * factor))
                probs_ref[head % 2, rows] = jnp.exp2(((scores - peak) * factor).astype(jnp.bfloat16))
                peak_ref[head, rows] = peak
            wide = jnp.concatenate([v_ref[:, cols], ones], axis=1)
            added = jnp.dot(probs_ref[head % 2], wide, preferred_element_type=jnp.float32)
            total_ref[head] = added if first else total_ref[head] * jnp.concatenate(scales, axis=0) + added

    for number, (k_ref, v_ref) in enumerate(blocks):
        if fresh and number == 0:
            one_block(True, k_ref, v_ref)
        else:
            pl.when(scalar_ref[flags[number]] == 1)(functools.partial(one_block, False, k_ref, v_ref))
    if last:
        for head in range(HEADS_HERE):
            total = total_ref[head]
            out_ref[:, head * HD : (head + 1) * HD] = (total[:, :HD] / total[:, HD:]).astype(jnp.bfloat16)


def attend(scalars, queries, flags, blocks, state=None, last=False):
    rows, width = queries.shape
    fresh = state is None
    share = rows // (NY * NXL * NC)
    tile = rows // NC
    count = len(flags)
    state_specs = [
        pl.BlockSpec((HEADS_HERE, tile, 1), lambda i, *_: (0, i, 0)),
        pl.BlockSpec((HEADS_HERE, tile, 2 * HD), lambda i, *_: (0, i, 0)),
    ]
    in_specs = [pl.BlockSpec((NY * NXL * NC, share, width), lambda i, *_: (0, 0, 0))]
    in_specs += [pl.BlockSpec(block.shape, lambda i, *_, rank=block.ndim: (0,) * rank) for block in blocks]
    operands = [queries.reshape(NY * NXL * NC, share, width), *blocks]
    if not fresh:
        in_specs += state_specs
        operands += state
    scratch = [pltpu.VMEM((2, tile, rows), jnp.bfloat16), pltpu.VMEM((2, tile, rows), jnp.float32)]
    if last:
        out_shape = jax.ShapeDtypeStruct((rows, width), jnp.bfloat16)
        out_specs = pl.BlockSpec((tile, width), lambda i, *_: (i, 0))
        scratch = [
            pltpu.VMEM((HEADS_HERE, tile, 2 * HD), jnp.float32),
            pltpu.VMEM((HEADS_HERE, tile, 1), jnp.float32),
            pltpu.VMEM((rows, width), jnp.bfloat16),
            pltpu.VMEM((rows, width), jnp.bfloat16),
        ] + scratch
    else:
        out_shape = [
            jax.ShapeDtypeStruct((HEADS_HERE, rows, 1), jnp.float32),
            jax.ShapeDtypeStruct((HEADS_HERE, rows, 2 * HD), jnp.float32),
        ]
        out_specs = state_specs
    return pl.pallas_call(
        functools.partial(attend_body, fresh, last, flags),
        out_shape=out_shape,
        grid_spec=pltpu.PrefetchScalarGridSpec(
            num_scalar_prefetch=1, grid=(NC,), in_specs=in_specs, out_specs=out_specs, scratch_shapes=scratch
        ),
        compiler_params=pltpu.CompilerParams(vmem_limit_bytes=40 * 1024 * 1024),
        cost_estimate=pl.CostEstimate(
            flops=4 * count * rows * rows * width, bytes_accessed=20 * rows * width, transcendentals=3 * count * rows * rows
        ),
    )(scalars, *operands)


def spread_clean(keys, values, root, z, xh, beside):
    rows, width = keys.shape
    own = jnp.stack([keys.reshape(NZ, rows // NZ, width), values.reshape(NZ, rows // NZ, width)], axis=1)
    distance = lax.rem(z - root // NXH + NZ, NZ)
    at_root = distance == 0
    beside = list(beside)
    up, down = own[4], own[5]
    for number in range(4):
        up = shift(jnp.where(at_root, own[4 - number], up) if number else up, "z", NZ, 1)
        if number < 3:
            down = shift(jnp.where(at_root, own[5 + number], down) if number else down, "z", NZ, -1)
        if number % 2:
            up, beside[number // 2] = lax.optimization_barrier((up, beside[number // 2]))
    piece = jnp.where(at_root, own[0], jnp.where(distance <= 4, up, down))
    piece = jnp.where(xh == lax.rem(root, NXH), piece, lax.ppermute(piece, "xh", SWAP))
    pieces = [piece]
    up = down = piece
    for number in range(4):
        up = shift(up, "z", NZ, 1)
        pieces.append(up)
        if number < 3:
            down = shift(down, "z", NZ, -1)
            pieces.append(down)
    return pieces, beside


def add(*terms):
    total = terms[0].astype(jnp.float32)
    for term in terms[1:]:
        total = total + term.astype(jnp.float32)
    return total


def sum_over_y(terms):
    half = terms[0].shape[-1] // 2
    from_below = shift(terms[2][..., :half], "y", NY, 1)
    from_above = shift(terms[2][..., half:], "y", NY, -1)
    rise = jnp.concatenate([add(terms[1][..., :half], from_below).astype(jnp.bfloat16), terms[1][..., half:]], axis=-1)
    fall = jnp.concatenate([terms[3][..., :half], add(terms[3][..., half:], from_above).astype(jnp.bfloat16)], axis=-1)
    return [terms[0], shift(rise, "y", NY, 1), shift(fall, "y", NY, -1)]


def local(queries, keys, values, residual, out_weight, gate_table, noise_steps, windows):
    z, xh, y, xl, core = (lax.axis_index(name) for name in ("z", "xh", "y", "xl", "c"))
    my_span = z * NXH + xh
    span_ids = lax.iota(jnp.int32, NZ * NXH)
    clean_root = jnp.sum(span_ids * (noise_steps == 0).astype(jnp.int32))
    rows, width = queries.shape
    share = residual.shape[0]

    beside = [shift(keys, "z", NZ, 1), shift(values, "z", NZ, 1)]
    pieces, (lag2_keys, lag2_values) = spread_clean(keys, values, clean_root, z, xh, beside)
    lag1_keys = lax.ppermute(jnp.where(xh == 0, keys, lag2_keys), "xh", SWAP)
    lag1_values = lax.ppermute(jnp.where(xh == 0, values, lag2_values), "xh", SWAP)
    weight = jnp.concatenate([out_weight, lax.ppermute(out_weight, "c", SWAP)], axis=0)

    scalars = jnp.stack(
        [
            jnp.int32(1),
            windows[my_span, 1],
            windows[my_span, 0],
            (my_span != clean_root).astype(jnp.int32),
            y,
            xl,
            core,
        ]
    )
    state = attend(scalars, queries, (0, 1), [keys, values, lag2_keys, lag2_values])
    state = attend(scalars, queries, (2,), [lag1_keys, lag1_values], state)
    state, weight = lax.optimization_barrier((state, weight))
    attended = attend(scalars, queries, (3,), pieces, state, last=True)
    taken = lax.ppermute(attended[rows // 2 :], "c", SWAP)
    both = jnp.concatenate([attended[: rows // 2], taken], axis=1)

    def project(low, high):
        terms = jnp.dot(both, weight[:, low:high], preferred_element_type=jnp.float32).astype(jnp.bfloat16)
        return terms.reshape(NXL, NY, share, high - low)

    x_first = project(0, X_FIRST)
    y_first = project(X_FIRST, out_weight.shape[1])

    x_got = lax.ppermute(x_first[1], "xl", SWAP)
    here = sum_over_y([y_first[:, number] for number in range(NY)])
    here_kept = [term[0] for term in here]
    here_sent = add(*[term[1] for term in here]).astype(jnp.bfloat16)
    here_got = lax.ppermute(here_sent, "xl", SWAP)
    x_sum = add(x_first[0], x_got).astype(jnp.bfloat16)
    left = add(*sum_over_y([x_sum[number] for number in range(NY)]))
    right = add(*here_kept, here_got)
    gate_row = lax.dynamic_slice_in_dim(gate_table, noise_steps[my_span], 1, 0)
    summed = jnp.concatenate([left, right], axis=1)
    return (residual.astype(jnp.float32) + gate_row * summed).astype(jnp.bfloat16)


def solution(mesh):
    fine = Mesh(mesh.devices.reshape(NZ, NXH, NY, NXL, NC), ("z", "xh", "y", "xl", "c"))
    span, mp = ("z", "xh"), ("y", "xl", "c")
    in_specs = (
        P(span, mp),
        P(span, mp),
        P(span, mp),
        P(span + mp, None),
        P(mp, None),
        P(),
        P(),
        P(),
    )
    out_specs = P(span + mp, None)
    return jax.shard_map(local, mesh=fine, in_specs=in_specs, out_specs=out_specs, check_vma=False)
```

time: 162 us -> 156 us (0.963)
  the two profiles are of different devices: /device:TPU:68 before, /device:TPU:24 now
where the time goes in v2:
time: 156 us
  waiting for transfers between devices  69.1 us (44%)
  starting transfers between devices  42.7 us (27%)
  Pallas kernels  19.1 us (12%)
  other arithmetic  11.1 us (7%)
  between operations  5.76 us (4%)
  matrix products  4.26 us (3%)
  local copies, waits for them, and re-layouts  3.73 us (2%)
    ppermute x24, waiting for transfers between devices, shift(): lax.ppermute(value, axis, [(i, (i + steps) % count) for i in range(count)])  53.6 us
    ppermute x24, starting transfers between devices, shift(): lax.ppermute(value, axis, [(i, (i + steps) % count) for i in range(count)])  32.2 us
    pallas_call x3, Pallas kernels, attend(): pl.pallas_call(functools.partial(attend_body, fresh, last, flags), out_sh...  19.1 us
    ppermute x1, waiting for transfers between devices, local(): x_got = lax.ppermute(x_first[1], 'xl', SWAP)  10.9 us
    concatenate x1, other arithmetic, local(): jnp.concatenate([out_weight, lax.ppermute(out_weight, 'c', SWAP)], axis=0)  4.85 us
    dot_general x2, matrix products, project(): jnp.dot(both, weight[:, low:high], preferred_element_type=jnp.float32)  4.26 us
  transfers between devices with their start and end apart: 31, of which 16 were waited for; matrix products, arithmetic and copies ran while one was open for 10% of the time, Pallas kernels for 8%

profile of v2, /device:TPU:24, one launch (start us, length us, event | category | flops | bytes accessed | tf_op | source)
XLA Modules:
  0.0 155.8 jit_solution(1294289708301575907)
XLA Ops:
  8.6 14.7 %collective-permute-done = bf16[2,96,384]{2,1,0:T(8,128)(2,1)S(1)} collective-permute-done((bf16[2,96,384]{2,1,0:T(8,128)(2,1)S(1)}, bf16[2,96,384]{2,1,0:T(8,128)(2,1)S(1)}, u32[]{:S(2)}, u32[]{:S(2)}) %collective-permute-start) | collective-permute-done | bytes 147488 | tf_op jit(solution)/shard_map/ppermute | solution.py:21
  23.5 3.2 %collective-permute-start.6 = (bf16[2,96,384]{2,1,0:T(8,128)(2,1)S(1)}, bf16[2,96,384]{2,1,0:T(8,128)(2,1)S(1)}, u32[]{:S(2)}, u32[]{:S(2)}) collective-permute-start(bf16[2,96,384]{2,1,0:T(8,128)(2,1)S(1)} %get-tuple-element.36), channel_id=1, source_target_pairs={{0,224},{32,0},{64,32},{96,64},{128,96},{160,128},{192,160},{224,1... | collective-permute-start | bytes 442376 | tf_op jit(solution)/shard_map/ppermute | solution.py:21
  26.7 3.6 %collective-permute-done.1 = bf16[2,96,384]{2,1,0:T(8,128)(2,1)S(1)} collective-permute-done((bf16[2,96,384]{2,1,0:T(8,128)(2,1)S(1)}, bf16[2,96,384]{2,1,0:T(8,128)(2,1)S(1)}, u32[]{:S(2)}, u32[]{:S(2)}) %collective-permute-start.1) | collective-permute-done | bytes 147488 | tf_op jit(solution)/shard_map/ppermute | solution.py:21
  30.4 3.2 %collective-permute-start.7 = (bf16[2,96,384]{2,1,0:T(8,128)(2,1)S(1)}, bf16[2,96,384]{2,1,0:T(8,128)(2,1)S(1)}, u32[]{:S(2)}, u32[]{:S(2)}) collective-permute-start(bf16[2,96,384]{2,1,0:T(8,128)(2,1)S(1)} %get-tuple-element.34), channel_id=1, source_target_pairs={{0,224},{32,0},{64,32},{96,64},{128,96},{160,128},{192,160},{224,1... | collective-permute-start | bytes 442376 | tf_op jit(solution)/shard_map/ppermute | solution.py:21
  33.6 4.1 %collective-permute-done.3 = bf16[2,96,384]{2,1,0:T(8,128)(2,1)S(1)} collective-permute-done((bf16[2,96,384]{2,1,0:T(8,128)(2,1)S(1)}, bf16[2,96,384]{2,1,0:T(8,128)(2,1)S(1)}, u32[]{:S(2)}, u32[]{:S(2)}) %collective-permute-start.3) | collective-permute-done | bytes 147488 | tf_op jit(solution)/shard_map/ppermute | solution.py:21
  41.9 3.0 %collective-permute-start.17 = (bf16[768,384]{1,0:T(8,128)(2,1)}, bf16[768,384]{1,0:T(8,128)(2,1)}, u32[]{:S(2)}, u32[]{:S(2)}) collective-permute-start(bf16[768,384]{1,0:T(8,128)(2,1)} %broadcast_select_fusion.1), channel_id=1, source_target_pairs={{0,16},{16,0},{1,17},{17,1},{2,18},{18,2},{3,19},{19,3},{4,20},{20... | collective-permute-start | bytes 1769480 | tf_op jit(solution)/shard_map/ppermute | solution.py:197
  45.0 6.0 %collective-permute-done.5.refs_5_ = bf16[768,384]{1,0:T(8,128)(2,1)S(1)} collective-permute-done((bf16[768,384]{1,0:T(8,128)(2,1)S(1)}, bf16[768,384]{1,0:T(8,128)(2,1)S(1)}, u32[]{:S(2)}, u32[]{:S(2)}) %collective-permute-start.5) | collective-permute-done | bytes 589856 | tf_op jit(solution)/shard_map/ppermute | solution.py:21
  52.6 3.1 %collective-permute-start.9 = (bf16[2,96,384]{2,1,0:T(8,128)(2,1)S(1)}, bf16[2,96,384]{2,1,0:T(8,128)(2,1)S(1)}, u32[]{:S(2)}, u32[]{:S(2)}) collective-permute-start(bf16[2,96,384]{2,1,0:T(8,128)(2,1)S(1)} %bitcast_select_fusion.5), channel_id=1, source_target_pairs={{0,16},{16,0},{1,17},{17,1},{2,18},{18,2},{3,19},{19,3},{4,20},{20... | collective-permute-start | bytes 442376 | tf_op jit(solution)/shard_map/ppermute | solution.py:159
  57.1 2.9 %collective-permute-done.9 = bf16[2,96,384]{2,1,0:T(8,128)(2,1)S(1)} collective-permute-done((bf16[2,96,384]{2,1,0:T(8,128)(2,1)S(1)}, bf16[2,96,384]{2,1,0:T(8,128)(2,1)S(1)}, u32[]{:S(2)}, u32[]{:S(2)}) %collective-permute-start.9) | collective-permute-done | bytes 147488 | tf_op jit(solution)/shard_map/ppermute | solution.py:159
  60.1 3.2 %collective-permute-start.11 = (bf16[2,96,384]{2,1,0:T(8,128)(2,1)S(1)}, bf16[2,96,384]{2,1,0:T(8,128)(2,1)}, u32[]{:S(2)}, u32[]{:S(2)}) collective-permute-start(bf16[2,96,384]{2,1,0:T(8,128)(2,1)S(1)} %broadcast_select_fusion.2.refs_2_), channel_id=1, source_target_pairs={{0,224},{32,0},{64,32},{96,64},{128,96},{160,128},{192,160},{224,1... | collective-permute-start | bytes 442376 | tf_op jit(solution)/shard_map/ppermute | solution.py:21
  63.4 3.2 %collective-permute-done.10.refs_3_ = bf16[2,96,384]{2,1,0:T(8,128)(2,1)} collective-permute-done((bf16[2,96,384]{2,1,0:T(8,128)(2,1)S(1)}, bf16[2,96,384]{2,1,0:T(8,128)(2,1)}, u32[]{:S(2)}, u32[]{:S(2)}) %collective-permute-start.10) | collective-permute-done | bytes 147488 | tf_op jit(solution)/shard_map/ppermute | solution.py:21
  71.9 3.5 %collective-permute-start.13 = (bf16[2,96,384]{2,1,0:T(8,128)(2,1)}, bf16[2,96,384]{2,1,0:T(8,128)(2,1)S(1)}, u32[]{:S(2)}, u32[]{:S(2)}) collective-permute-start(bf16[2,96,384]{2,1,0:T(8,128)(2,1)} %collective-permute-done.11.refs_4_), channel_id=1, source_target_pairs={{0,224},{32,0},{64,32},{96,64},{128,96},{160,128},{192,160},{224,1... | collective-permute-start | bytes 442376 | tf_op jit(solution)/shard_map/ppermute | solution.py:21
  75.4 7.3 %shard_map.82 = (f32[3,768,1]{2,1,0:T(8,128)S(1)}, f32[3,768,256]{2,1,0:T(8,128)S(1)}) custom-call(s32[7]{0:T(128)S(1)} %stack.26.refs_0_, bf16[16,48,384]{2,1,0:T(8,128)(2,1)S(1)} %bitcast.92, bf16[768,384]{1,0:T(8,128)(2,1)S(1)} %copy-done.2, bf16[768,384]{1,0:T(8,128)(2,1)S(1)} %copy-done.1, bf16[768,384]{1,0:T(8,128)(2,1)S(1)} %collective-permute-done.2.refs_4_, ...), custom_call_target="tpu_custom_call" | custom-call | flops 1811939328 | bytes 5898240 | tf_op jit(solution)/shard_map/pallas_call | solution.py:132
  84.8 6.0 %shard_map.83 = (f32[3,768,1]{2,1,0:T(8,128)S(1)}, f32[3,768,256]{2,1,0:T(8,128)S(1)}) custom-call(s32[7]{0:T(128)S(1)} %stack.26.refs_0_, bf16[16,48,384]{2,1,0:T(8,128)(2,1)S(1)} %bitcast.93, bf16[768,384]{1,0:T(8,128)(2,1)} %collective-permute-done.17.refs_2_, bf16[768,384]{1,0:T(8,128)(2,1)} %collective-permute-done.18.refs_3_, ...), custom_call_target="tpu_custom_call" | custom-call | flops 905969664 | bytes 5898240 | tf_op jit(solution)/shard_map/pallas_call | solution.py:132
  90.7 4.9 %pad_maximum_fusion = bf16[768,6144]{1,0:T(8,128)(2,1)S(1)} fusion(bf16[384,6144]{1,0:T(8,128)(2,1)} %collective-permute-done.19, bf16[384,6144]{1,0:T(8,128)(2,1)} %param.12), kind=kLoop, calls=%fused_computation | loop fusion | flops 18874368 | bytes 18874368 | tf_op jit(solution)/shard_map/concatenate | solution.py:199
  95.6 5.9 %shard_map.84 = bf16[768,384]{1,0:T(8,128)(2,1)S(1)} custom-call(s32[7]{0:T(128)S(1)} %stack.26.refs_0_, bf16[16,48,384]{2,1,0:T(8,128)(2,1)S(1)} %bitcast.94, bf16[2,96,384]{2,1,0:T(8,128)(2,1)S(1)} %broadcast_select_fusion.2.refs_2_, bf16[2,96,384]{2,1,0:T(8,128)(2,1)} %collective-permute-done.10.refs_3_, ...), custom_call_target="tpu_custom_call" | custom-call | flops 905969664 | bytes 5898240 | tf_op jit(solution)/shard_map/pallas_call | solution.py:132
  108.5 2.8 %collective-permute-start.21 = (bf16[4,48,2688]{2,1,0:T(8,128)(2,1)S(1)}, bf16[4,48,2688]{2,1,0:T(8,128)(2,1)S(1)}, u32[]{:S(2)}, u32[]{:S(2)}) collective-permute-start(bf16[4,48,2688]{2,1,0:T(8,128)(2,1)S(1)} %bitcast.99), channel_id=1, source_target_pairs={{0,2},{2,0},{1,3},{3,1},{4,6},{6,4},{5,7},{7,5},{8,10},{10,8},{9,1... | collective-permute-start | bytes 3096584 | tf_op jit(solution)/shard_map/ppermute | solution.py:226
  113.4 2.9 %collective-permute-done.26 = bf16[2,48,1728]{2,1,0:T(8,128)(2,1)S(1)} collective-permute-done((bf16[2,48,1728]{2,1,0:T(8,128)(2,1)S(1)}, bf16[2,48,1728]{2,1,0:T(8,128)(2,1)S(1)}, u32[]{:S(2)}, u32[]{:S(2)}) %collective-permute-start.26) | collective-permute-done | bytes 331808 | tf_op jit(solution)/shard_map/ppermute | solution.py:21
  118.2 4.2 %collective-permute-done.28 = bf16[2,48,1728]{2,1,0:T(8,128)(2,1)S(1)} collective-permute-done((bf16[2,48,1728]{2,1,0:T(8,128)(2,1)S(1)}, bf16[2,48,1728]{2,1,0:T(8,128)(2,1)S(1)}, u32[]{:S(2)}, u32[]{:S(2)}) %collective-permute-start.28) | collective-permute-done | bytes 331808 | tf_op jit(solution)/shard_map/ppermute | solution.py:21
  123.3 10.9 %collective-permute-done.21 = bf16[4,48,2688]{2,1,0:T(8,128)(2,1)S(1)} collective-permute-done((bf16[4,48,2688]{2,1,0:T(8,128)(2,1)S(1)}, bf16[4,48,2688]{2,1,0:T(8,128)(2,1)S(1)}, u32[]{:S(2)}, u32[]{:S(2)}) %collective-permute-start.21) | collective-permute-done | bytes 1032224 | tf_op jit(solution)/shard_map/ppermute | solution.py:226
  136.3 3.3 %collective-permute-done.29 = bf16[2,48,3456]{2,1,0:T(8,128)(2,1)S(1)} collective-permute-done((bf16[2,48,3456]{2,1,0:T(8,128)(2,1)S(1)}, bf16[2,48,3456]{2,1,0:T(8,128)(2,1)S(1)}, u32[]{:S(2)}, u32[]{:S(2)}) %collective-permute-start.29) | collective-permute-done | bytes 663584 | tf_op jit(solution)/shard_map/ppermute | solution.py:21
  140.8 3.3 %collective-permute-start.23 = (bf16[48,2688]{1,0:T(8,128)(2,1)S(1)}, bf16[48,2688]{1,0:T(8,128)(2,1)S(1)}, u32[]{:S(2)}, u32[]{:S(2)}) collective-permute-start(bf16[48,2688]{1,0:T(8,128)(2,1)S(1)} %pad_maximum_fusion.6), channel_id=1, source_target_pairs={{0,4},{4,8},{8,12},{12,0},{1,5},{5,9},{9,13},{13,1},{2,6},{6,10},{... | collective-permute-start | bytes 774152 | tf_op jit(solution)/shard_map/ppermute | solution.py:21
  144.1 2.7 %collective-permute-done.24 = bf16[48,1344]{1,0:T(8,128)(2,1)S(1)} collective-permute-done((bf16[48,1344]{1,0:T(8,128)(2,1)S(1)}, bf16[48,1344]{1,0:T(8,128)(2,1)S(1)}, u32[]{:S(2)}, u32[]{:S(2)}) %collective-permute-start.24) | collective-permute-done | bytes 129056 | tf_op jit(solution)/shard_map/ppermute | solution.py:21
  148.0 6.7 %collective-permute-done.25 = bf16[48,2688]{1,0:T(8,128)(2,1)S(1)} collective-permute-done((bf16[48,2688]{1,0:T(8,128)(2,1)S(1)}, bf16[48,2688]{1,0:T(8,128)(2,1)S(1)}, u32[]{:S(2)}, u32[]{:S(2)}) %collective-permute-start.25) | collective-permute-done | bytes 258080 | tf_op jit(solution)/shard_map/ppermute | solution.py:21
  (94 shorter events, 35.4 us)
Async XLA Ops:
  0.0 90.7 %collective-permute-start.19 = (bf16[384,6144]{1,0:T(8,128)(2,1)}, bf16[384,6144]{1,0:T(8,128)(2,1)}, u32[]{:S(2)}, u32[]{:S(2)}) collective-permute-start(bf16[384,6144]{1,0:T(8,128)(2,1)} %param.12), channel_id=1, source_target_pairs={{0,1},{1,0},{2,3},{3,2},{4,5},{5,4},{6,7},{7,6},{8,9},{9,8},{10,11... | collective-permute-start | bytes 14155784 | tf_op jit(solution)/shard_map/ppermute | solution.py:199
  0.1 30.1 %collective-permute-start.2 = (bf16[768,384]{1,0:T(8,128)(2,1)}, bf16[768,384]{1,0:T(8,128)(2,1)S(1)}, u32[]{:S(2)}, u32[]{:S(2)}) collective-permute-start(bf16[768,384]{1,0:T(8,128)(2,1)} %refs_2_.1), channel_id=1, source_target_pairs={{0,32},{32,64},{64,96},{96,128},{128,160},{160,192},{192,224},{224... | collective-permute-start | bytes 1769480 | tf_op jit(solution)/shard_map/ppermute | solution.py:21
  3.1 20.2 %collective-permute-start = (bf16[2,96,384]{2,1,0:T(8,128)(2,1)S(1)}, bf16[2,96,384]{2,1,0:T(8,128)(2,1)S(1)}, u32[]{:S(2)}, u32[]{:S(2)}) collective-permute-start(bf16[2,96,384]{2,1,0:T(8,128)(2,1)S(1)} %get-tuple-element.37), channel_id=1, source_target_pairs={{0,32},{32,64},{64,96},{96,128},{128,160},{160,192},{192,224},{224... | collective-permute-start | bytes 442376 | tf_op jit(solution)/shard_map/ppermute | solution.py:21
  30.3 7.4 %collective-permute-start.3 = (bf16[2,96,384]{2,1,0:T(8,128)(2,1)S(1)}, bf16[2,96,384]{2,1,0:T(8,128)(2,1)S(1)}, u32[]{:S(2)}, u32[]{:S(2)}) collective-permute-start(bf16[2,96,384]{2,1,0:T(8,128)(2,1)S(1)} %get-tuple-element.35), channel_id=1, source_target_pairs={{0,32},{32,64},{64,96},{96,128},{128,160},{160,192},{192,224},{224... | collective-permute-start | bytes 442376 | tf_op jit(solution)/shard_map/ppermute | solution.py:21
  30.4 7.3 %collective-permute-start.7 = (bf16[2,96,384]{2,1,0:T(8,128)(2,1)S(1)}, bf16[2,96,384]{2,1,0:T(8,128)(2,1)S(1)}, u32[]{:S(2)}, u32[]{:S(2)}) collective-permute-start(bf16[2,96,384]{2,1,0:T(8,128)(2,1)S(1)} %get-tuple-element.34), channel_id=1, source_target_pairs={{0,224},{32,0},{64,32},{96,64},{128,96},{160,128},{192,160},{224,1... | collective-permute-start | bytes 442376 | tf_op jit(solution)/shard_map/ppermute | solution.py:21
  33.6 17.3 %collective-permute-start.5 = (bf16[768,384]{1,0:T(8,128)(2,1)S(1)}, bf16[768,384]{1,0:T(8,128)(2,1)S(1)}, u32[]{:S(2)}, u32[]{:S(2)}) collective-permute-start(bf16[768,384]{1,0:T(8,128)(2,1)S(1)} %copy-done.1), channel_id=1, source_target_pairs={{0,32},{32,64},{64,96},{96,128},{128,160},{160,192},{192,224},{224... | collective-permute-start | bytes 1769480 | tf_op jit(solution)/shard_map/ppermute | solution.py:21
  37.7 14.8 %collective-permute-start.4 = (bf16[2,96,384]{2,1,0:T(8,128)(2,1)S(1)}, bf16[2,96,384]{2,1,0:T(8,128)(2,1)S(1)}, u32[]{:S(2)}, u32[]{:S(2)}) collective-permute-start(bf16[2,96,384]{2,1,0:T(8,128)(2,1)S(1)} %get-tuple-element.33), channel_id=1, source_target_pairs={{0,32},{32,64},{64,96},{96,128},{128,160},{160,192},{192,224},{224... | collective-permute-start | bytes 442376 | tf_op jit(solution)/shard_map/ppermute | solution.py:21
  39.2 13.4 %collective-permute-start.8 = (bf16[2,96,384]{2,1,0:T(8,128)(2,1)S(1)}, bf16[2,96,384]{2,1,0:T(8,128)(2,1)S(1)}, u32[]{:S(2)}, u32[]{:S(2)}) collective-permute-start(bf16[2,96,384]{2,1,0:T(8,128)(2,1)S(1)} %get-tuple-element.32), channel_id=1, source_target_pairs={{0,224},{32,0},{64,32},{96,64},{128,96},{160,128},{192,160},{224,1... | collective-permute-start | bytes 442376 | tf_op jit(solution)/shard_map/ppermute | solution.py:21
  41.9 42.8 %collective-permute-start.17 = (bf16[768,384]{1,0:T(8,128)(2,1)}, bf16[768,384]{1,0:T(8,128)(2,1)}, u32[]{:S(2)}, u32[]{:S(2)}) collective-permute-start(bf16[768,384]{1,0:T(8,128)(2,1)} %broadcast_select_fusion.1), channel_id=1, source_target_pairs={{0,16},{16,0},{1,17},{17,1},{2,18},{18,2},{3,19},{19,3},{4,20},{20... | collective-permute-start | bytes 1769480 | tf_op jit(solution)/shard_map/ppermute | solution.py:197
  52.6 7.4 %collective-permute-start.9 = (bf16[2,96,384]{2,1,0:T(8,128)(2,1)S(1)}, bf16[2,96,384]{2,1,0:T(8,128)(2,1)S(1)}, u32[]{:S(2)}, u32[]{:S(2)}) collective-permute-start(bf16[2,96,384]{2,1,0:T(8,128)(2,1)S(1)} %bitcast_select_fusion.5), channel_id=1, source_target_pairs={{0,16},{16,0},{1,17},{17,1},{2,18},{18,2},{3,19},{19,3},{4,20},{20... | collective-permute-start | bytes 442376 | tf_op jit(solution)/shard_map/ppermute | solution.py:159
  56.6 28.2 %collective-permute-start.18 = (bf16[768,384]{1,0:T(8,128)(2,1)}, bf16[768,384]{1,0:T(8,128)(2,1)}, u32[]{:S(2)}, u32[]{:S(2)}) collective-permute-start(bf16[768,384]{1,0:T(8,128)(2,1)} %broadcast_select_fusion), channel_id=1, source_target_pairs={{0,16},{16,0},{1,17},{17,1},{2,18},{18,2},{3,19},{19,3},{4,20},{20... | collective-permute-start | bytes 1769480 | tf_op jit(solution)/shard_map/ppermute | solution.py:198
  60.1 11.8 %collective-permute-start.11 = (bf16[2,96,384]{2,1,0:T(8,128)(2,1)S(1)}, bf16[2,96,384]{2,1,0:T(8,128)(2,1)}, u32[]{:S(2)}, u32[]{:S(2)}) collective-permute-start(bf16[2,96,384]{2,1,0:T(8,128)(2,1)S(1)} %broadcast_select_fusion.2.refs_2_), channel_id=1, source_target_pairs={{0,224},{32,0},{64,32},{96,64},{128,96},{160,128},{192,160},{224,1... | collective-permute-start | bytes 442376 | tf_op jit(solution)/shard_map/ppermute | solution.py:21
  66.6 8.8 %collective-permute-start.12 = (bf16[2,96,384]{2,1,0:T(8,128)(2,1)}, bf16[2,96,384]{2,1,0:T(8,128)(2,1)}, u32[]{:S(2)}, u32[]{:S(2)}) collective-permute-start(bf16[2,96,384]{2,1,0:T(8,128)(2,1)} %collective-permute-done.10.refs_3_), channel_id=1, source_target_pairs={{0,32},{32,64},{64,96},{96,128},{128,160},{160,192},{192,224},{224... | collective-permute-start | bytes 442376 | tf_op jit(solution)/shard_map/ppermute | solution.py:21
  71.9 10.8 %collective-permute-start.13 = (bf16[2,96,384]{2,1,0:T(8,128)(2,1)}, bf16[2,96,384]{2,1,0:T(8,128)(2,1)S(1)}, u32[]{:S(2)}, u32[]{:S(2)}) collective-permute-start(bf16[2,96,384]{2,1,0:T(8,128)(2,1)} %collective-permute-done.11.refs_4_), channel_id=1, source_target_pairs={{0,224},{32,0},{64,32},{96,64},{128,96},{160,128},{192,160},{224,1... | collective-permute-start | bytes 442376 | tf_op jit(solution)/shard_map/ppermute | solution.py:21
  75.4 7.4 %collective-permute-start.14 = (bf16[2,96,384]{2,1,0:T(8,128)(2,1)}, bf16[2,96,384]{2,1,0:T(8,128)(2,1)S(1)}, u32[]{:S(2)}, u32[]{:S(2)}) collective-permute-start(bf16[2,96,384]{2,1,0:T(8,128)(2,1)} %collective-permute-done.12.refs_5_), channel_id=1, source_target_pairs={{0,32},{32,64},{64,96},{96,128},{128,160},{160,192},{192,224},{224... | collective-permute-start | bytes 442376 | tf_op jit(solution)/shard_map/ppermute | solution.py:21
  82.6 13.0 %collective-permute-start.15 = (bf16[2,96,384]{2,1,0:T(8,128)(2,1)S(1)}, bf16[2,96,384]{2,1,0:T(8,128)(2,1)S(1)}, u32[]{:S(2)}, u32[]{:S(2)}) collective-permute-start(bf16[2,96,384]{2,1,0:T(8,128)(2,1)S(1)} %collective-permute-done.13.refs_6_), channel_id=1, source_target_pairs={{0,224},{32,0},{64,32},{96,64},{128,96},{160,128},{192,160},{224,1... | collective-permute-start | bytes 442376 | tf_op jit(solution)/shard_map/ppermute | solution.py:21
  82.8 12.9 %collective-permute-start.16 = (bf16[2,96,384]{2,1,0:T(8,128)(2,1)S(1)}, bf16[2,96,384]{2,1,0:T(8,128)(2,1)S(1)}, u32[]{:S(2)}, u32[]{:S(2)}) collective-permute-start(bf16[2,96,384]{2,1,0:T(8,128)(2,1)S(1)} %collective-permute-done.14.refs_7_), channel_id=1, source_target_pairs={{0,32},{32,64},{64,96},{96,128},{128,160},{160,192},{192,224},{224... | collective-permute-start | bytes 442376 | tf_op jit(solution)/shard_map/ppermute | solution.py:21
  106.2 10.2 %collective-permute-start.26 = (bf16[2,48,1728]{2,1,0:T(8,128)(2,1)S(1)}, bf16[2,48,1728]{2,1,0:T(8,128)(2,1)S(1)}, u32[]{:S(2)}, u32[]{:S(2)}) collective-permute-start(bf16[2,48,1728]{2,1,0:T(8,128)(2,1)S(1)} %get-tuple-element.41), channel_id=1, source_target_pairs={{0,4},{4,8},{8,12},{12,0},{1,5},{5,9},{9,13},{13,1},{2,6},{6,10},{... | collective-permute-start | bytes 995336 | tf_op jit(solution)/shard_map/ppermute | solution.py:21
  108.5 25.7 %collective-permute-start.21 = (bf16[4,48,2688]{2,1,0:T(8,128)(2,1)S(1)}, bf16[4,48,2688]{2,1,0:T(8,128)(2,1)S(1)}, u32[]{:S(2)}, u32[]{:S(2)}) collective-permute-start(bf16[4,48,2688]{2,1,0:T(8,128)(2,1)S(1)} %bitcast.99), channel_id=1, source_target_pairs={{0,2},{2,0},{1,3},{3,1},{4,6},{6,4},{5,7},{7,5},{8,10},{10,8},{9,1... | collective-permute-start | bytes 3096584 | tf_op jit(solution)/shard_map/ppermute | solution.py:226
  111.5 10.9 %collective-permute-start.28 = (bf16[2,48,1728]{2,1,0:T(8,128)(2,1)S(1)}, bf16[2,48,1728]{2,1,0:T(8,128)(2,1)S(1)}, u32[]{:S(2)}, u32[]{:S(2)}) collective-permute-start(bf16[2,48,1728]{2,1,0:T(8,128)(2,1)S(1)} %get-tuple-element.42), channel_id=1, source_target_pairs={{0,12},{4,0},{8,4},{12,8},{1,13},{5,1},{9,5},{13,9},{2,14},{6,2},{... | collective-permute-start | bytes 995336 | tf_op jit(solution)/shard_map/ppermute | solution.py:21
  116.6 19.7 %collective-permute-start.27 = (bf16[2,48,3456]{2,1,0:T(8,128)(2,1)S(1)}, bf16[2,48,3456]{2,1,0:T(8,128)(2,1)S(1)}, u32[]{:S(2)}, u32[]{:S(2)}) collective-permute-start(bf16[2,48,3456]{2,1,0:T(8,128)(2,1)S(1)} %pad_maximum_fusion.1), channel_id=1, source_target_pairs={{0,4},{4,8},{8,12},{12,0},{1,5},{5,9},{9,13},{13,1},{2,6},{6,10},{... | collective-permute-start | bytes 1990664 | tf_op jit(solution)/shard_map/ppermute | solution.py:21
  122.7 16.9 %collective-permute-start.29 = (bf16[2,48,3456]{2,1,0:T(8,128)(2,1)S(1)}, bf16[2,48,3456]{2,1,0:T(8,128)(2,1)S(1)}, u32[]{:S(2)}, u32[]{:S(2)}) collective-permute-start(bf16[2,48,3456]{2,1,0:T(8,128)(2,1)S(1)} %pad_maximum_fusion.2), channel_id=1, source_target_pairs={{0,12},{4,0},{8,4},{12,8},{1,13},{5,1},{9,5},{13,9},{2,14},{6,2},{... | collective-permute-start | bytes 1990664 | tf_op jit(solution)/shard_map/ppermute | solution.py:21
  139.7 7.6 %collective-permute-start.30 = (bf16[48,3456]{1,0:T(8,128)(2,1)S(1)}, bf16[48,3456]{1,0:T(8,128)(2,1)S(1)}, u32[]{:S(2)}, u32[]{:S(2)}) collective-permute-start(bf16[48,3456]{1,0:T(8,128)(2,1)S(1)} %fusion.5), channel_id=1, source_target_pairs={{0,2},{2,0},{1,3},{3,1},{4,6},{6,4},{5,7},{7,5},{8,10},{10,8},{9,1... | collective-permute-start | bytes 995336 | tf_op jit(solution)/shard_map/ppermute | solution.py:230
  147.1 7.6 %collective-permute-start.25 = (bf16[48,2688]{1,0:T(8,128)(2,1)S(1)}, bf16[48,2688]{1,0:T(8,128)(2,1)S(1)}, u32[]{:S(2)}, u32[]{:S(2)}) collective-permute-start(bf16[48,2688]{1,0:T(8,128)(2,1)S(1)} %pad_maximum_fusion.7), channel_id=1, source_target_pairs={{0,12},{4,0},{8,4},{12,8},{1,13},{5,1},{9,5},{13,9},{2,14},{6,2},{... | collective-permute-start | bytes 774152 | tf_op jit(solution)/shard_map/ppermute | solution.py:21
  (14 other events, 243.0 us)

commit v3 on v2

--- a/solution.py
+++ b/solution.py
@@ -142,30 +142,46 @@
     )(scalars, *operands)
 
 
-def spread_clean(keys, values, root, z, xh, beside):
+def fetch(keys, values, root, z, xh, weight, first_pass):
     rows, width = keys.shape
-    own = jnp.stack([keys.reshape(NZ, rows // NZ, width), values.reshape(NZ, rows // NZ, width)], axis=1)
+    cut = rows // NZ
+    own = jnp.stack([keys.reshape(NZ, cut, width), values.reshape(NZ, cut, width)], axis=1)
     distance = lax.rem(z - root // NXH + NZ, NZ)
     at_root = distance == 0
-    beside = list(beside)
-    up, down = own[4], own[5]
-    for number in range(4):
-        up = shift(jnp.where(at_root, own[4 - number], up) if number else up, "z", NZ, 1)
-        if number < 3:
-            down = shift(jnp.where(at_root, own[5 + number], down) if number else down, "z", NZ, -1)
-        if number % 2:
-            up, beside[number // 2] = lax.optimization_barrier((up, beside[number // 2]))
-    piece = jnp.where(at_root, own[0], jnp.where(distance <= 4, up, down))
+    up = shift(own[2], "z", NZ, 1)
+    keys_late, up = lax.optimization_barrier((keys, up))
+    lag2_keys = shift(keys_late, "z", NZ, 1)
+    up = shift(jnp.where(at_root, own[1], up), "z", NZ, 1)
+    values_late, up = lax.optimization_barrier((values, up))
+    lag2_values = shift(values_late, "z", NZ, 1)
+    down = shift(own[3], "z", NZ, -1)
+    for number in range(4, NZ):
+        if number == 5:
+            down, _ = lax.optimization_barrier((down, up))
+        if number == 6:
+            down, lag2_keys = lax.optimization_barrier((down, lag2_keys))
+        down = shift(jnp.where(at_root, own[number], down), "z", NZ, -1)
+    lag1_keys = lax.ppermute(jnp.where(xh == 0, keys, lag2_keys), "xh", SWAP)
+    piece = jnp.where(at_root, own[0], jnp.where(distance <= 2, up, down))
+    piece, lag1_keys = lax.optimization_barrier((piece, lag1_keys))
     piece = jnp.where(xh == lax.rem(root, NXH), piece, lax.ppermute(piece, "xh", SWAP))
+    piece, lag2_values = lax.optimization_barrier((piece, lag2_values))
+    lag1_values = lax.ppermute(jnp.where(xh == 0, values, lag2_values), "xh", SWAP)
+    peak, total = first_pass([lag2_keys, lag2_values])
     pieces = [piece]
     up = down = piece
     for number in range(4):
+        if number == 1:
+            up, peak = lax.optimization_barrier((up, peak))
+        if number == 2:
+            peak, weight = lax.optimization_barrier((peak, weight))
+            up, peak = lax.optimization_barrier((up, peak))
         up = shift(up, "z", NZ, 1)
         pieces.append(up)
         if number < 3:
             down = shift(down, "z", NZ, -1)
             pieces.append(down)
-    return pieces, beside
+    return [peak, total], [lag1_keys, lag1_values], pieces, weight
 
 
 def add(*terms):
@@ -192,12 +208,7 @@
     rows, width = queries.shape
     share = residual.shape[0]
 
-    beside = [shift(keys, "z", NZ, 1), shift(values, "z", NZ, 1)]
-    pieces, (lag2_keys, lag2_values) = spread_clean(keys, values, clean_root, z, xh, beside)
-    lag1_keys = lax.ppermute(jnp.where(xh == 0, keys, lag2_keys), "xh", SWAP)
-    lag1_values = lax.ppermute(jnp.where(xh == 0, values, lag2_values), "xh", SWAP)
     weight = jnp.concatenate([out_weight, lax.ppermute(out_weight, "c", SWAP)], axis=0)
-
     scalars = jnp.stack(
         [
             jnp.int32(1),
@@ -209,9 +220,11 @@
             core,
         ]
     )
-    state = attend(scalars, queries, (0, 1), [keys, values, lag2_keys, lag2_values])
-    state = attend(scalars, queries, (2,), [lag1_keys, lag1_values], state)
-    state, weight = lax.optimization_barrier((state, weight))
+    def first_pass(lag2):
+        return attend(scalars, queries, (0, 1), [keys, values, *lag2])
+
+    state, lag1, pieces, weight = fetch(keys, values, clean_root, z, xh, weight, first_pass)
+    state = attend(scalars, queries, (2,), lag1, state)
     attended = attend(scalars, queries, (3,), pieces, state, last=True)
     taken = lax.ppermute(attended[rows // 2 :], "c", SWAP)
     both = jnp.concatenate([attended[: rows // 2], taken], axis=1)

time: 156 us -> 165 us (1.058)
  the two profiles are of different devices: /device:TPU:24 before, /device:TPU:120 now
where the time goes in v3:
time: 165 us
  waiting for transfers between devices  65.8 us (40%)
  starting transfers between devices  50.5 us (31%)
  Pallas kernels  15.7 us (10%)
  other arithmetic  13.9 us (8%)
  local copies, waits for them, and re-layouts  9.16 us (6%)
  between operations  5.5 us (3%)
  matrix products  4.34 us (3%)
    ppermute x24, waiting for transfers between devices, shift(): lax.ppermute(value, axis, [(i, (i + steps) % count) for i in range(count)])  48 us
    ppermute x24, starting transfers between devices, shift(): lax.ppermute(value, axis, [(i, (i + steps) % count) for i in range(count)])  38.8 us
    pallas_call x3, Pallas kernels, attend(): pl.pallas_call(functools.partial(attend_body, fresh, last, flags), out_sh...  15.7 us
    ppermute x1, waiting for transfers between devices, local(): x_got = lax.ppermute(x_first[1], 'xl', SWAP)  12.2 us
    concatenate x1, other arithmetic, local(): jnp.concatenate([out_weight, lax.ppermute(out_weight, 'c', SWAP)], axis=0)  6.62 us
    unnamed x48, local copies, waits for them, and re-layouts  5.58 us
    dot_general x2, matrix products, project(): jnp.dot(both, weight[:, low:high], preferred_element_type=jnp.float32)  4.34 us
  transfers between devices with their start and end apart: 31, of which 16 were waited for; matrix products, arithmetic and copies ran while one was open for 11% of the time, Pallas kernels for 6%

profile of v3, /device:TPU:120, one launch (start us, length us, event | category | flops | bytes accessed | tf_op | source)
XLA Modules:
  0.0 164.8 jit_solution(4739134511855392743)
XLA Ops:
  1.3 3.2 %collective-permute-start = (bf16[2,96,384]{2,1,0:T(8,128)(2,1)S(1)}, bf16[2,96,384]{2,1,0:T(8,128)(2,1)S(1)}, u32[]{:S(2)}, u32[]{:S(2)}) collective-permute-start(bf16[2,96,384]{2,1,0:T(8,128)(2,1)S(1)} %get-tuple-element.55), channel_id=1, source_target_pairs={{0,32},{32,64},{64,96},{96,128},{128,160},{160,192},{192,224},{224... | collective-permute-start | bytes 442376 | tf_op jit(solution)/shard_map/ppermute | solution.py:21
  8.2 3.7 %collective-permute-start.5 = (bf16[768,384]{1,0:T(8,128)(2,1)S(1)}, bf16[768,384]{1,0:T(8,128)(2,1)S(1)}, u32[]{:S(2)}, u32[]{:S(2)}) collective-permute-start(bf16[768,384]{1,0:T(8,128)(2,1)S(1)} %copy-done.2), channel_id=1, source_target_pairs={{0,32},{32,64},{64,96},{96,128},{128,160},{160,192},{192,224},{224... | collective-permute-start | bytes 1769480 | tf_op jit(solution)/shard_map/ppermute | solution.py:21
  14.0 13.4 %collective-permute-done.1 = bf16[2,96,384]{2,1,0:T(8,128)(2,1)} collective-permute-done((bf16[2,96,384]{2,1,0:T(8,128)(2,1)S(1)}, bf16[2,96,384]{2,1,0:T(8,128)(2,1)}, u32[]{:S(2)}, u32[]{:S(2)}) %collective-permute-start.1) | collective-permute-done | bytes 147488 | tf_op jit(solution)/shard_map/ppermute | solution.py:21
  27.5 6.9 %collective-permute-done.4 = bf16[2,96,384]{2,1,0:T(8,128)(2,1)S(1)} collective-permute-done((bf16[2,96,384]{2,1,0:T(8,128)(2,1)S(1)}, bf16[2,96,384]{2,1,0:T(8,128)(2,1)S(1)}, u32[]{:S(2)}, u32[]{:S(2)}) %collective-permute-start.4) | collective-permute-done | bytes 147488 | tf_op jit(solution)/shard_map/ppermute | solution.py:21
  35.5 3.0 %collective-permute-start.8 = (bf16[768,384]{1,0:T(8,128)(2,1)}, bf16[768,384]{1,0:T(8,128)(2,1)S(1)}, u32[]{:S(2)}, u32[]{:S(2)}) collective-permute-start(bf16[768,384]{1,0:T(8,128)(2,1)} %broadcast_select_fusion.1), channel_id=1, source_target_pairs={{0,16},{16,0},{1,17},{17,1},{2,18},{18,2},{3,19},{19,3},{4,20},{20... | collective-permute-start | bytes 1769480 | tf_op jit(solution)/shard_map/ppermute | solution.py:164
  41.0 3.2 %collective-permute-start.10 = (bf16[768,384]{1,0:T(8,128)(2,1)S(1)}, bf16[768,384]{1,0:T(8,128)(2,1)S(1)}, u32[]{:S(2)}, u32[]{:S(2)}) collective-permute-start(bf16[768,384]{1,0:T(8,128)(2,1)S(1)} %copy-done.1), channel_id=1, source_target_pairs={{0,32},{32,64},{64,96},{96,128},{128,160},{160,192},{192,224},{224... | collective-permute-start | bytes 1769480 | tf_op jit(solution)/shard_map/ppermute | solution.py:21
  44.2 3.1 %collective-permute-done.7 = bf16[2,96,384]{2,1,0:T(8,128)(2,1)S(1)} collective-permute-done((bf16[2,96,384]{2,1,0:T(8,128)(2,1)S(1)}, bf16[2,96,384]{2,1,0:T(8,128)(2,1)S(1)}, u32[]{:S(2)}, u32[]{:S(2)}) %collective-permute-start.7) | collective-permute-done | bytes 147488 | tf_op jit(solution)/shard_map/ppermute | solution.py:21
  47.4 2.9 %collective-permute-done.8.refs_2_ = bf16[768,384]{1,0:T(8,128)(2,1)S(1)} collective-permute-done((bf16[768,384]{1,0:T(8,128)(2,1)}, bf16[768,384]{1,0:T(8,128)(2,1)S(1)}, u32[]{:S(2)}, u32[]{:S(2)}) %collective-permute-start.8) | collective-permute-done | bytes 589856 | tf_op jit(solution)/shard_map/ppermute | solution.py:164
  50.3 3.0 %collective-permute-start.9 = (bf16[2,96,384]{2,1,0:T(8,128)(2,1)S(1)}, bf16[2,96,384]{2,1,0:T(8,128)(2,1)}, u32[]{:S(2)}, u32[]{:S(2)}) collective-permute-start(bf16[2,96,384]{2,1,0:T(8,128)(2,1)S(1)} %bitcast_select_fusion.5), channel_id=1, source_target_pairs={{0,16},{16,0},{1,17},{17,1},{2,18},{18,2},{3,19},{19,3},{4,20},{20... | collective-permute-start | bytes 442376 | tf_op jit(solution)/shard_map/ppermute | solution.py:167
  58.0 3.0 %collective-permute-start.11 = (bf16[2,96,384]{2,1,0:T(8,128)(2,1)S(1)}, bf16[2,96,384]{2,1,0:T(8,128)(2,1)S(1)}, u32[]{:S(2)}, u32[]{:S(2)}) collective-permute-start(bf16[2,96,384]{2,1,0:T(8,128)(2,1)S(1)} %broadcast_select_fusion.2.refs_2_), channel_id=1, source_target_pairs={{0,32},{32,64},{64,96},{96,128},{128,160},{160,192},{192,224},{224... | collective-permute-start | bytes 442376 | tf_op jit(solution)/shard_map/ppermute | solution.py:21
  61.9 3.0 %collective-permute-start.19 = (bf16[768,384]{1,0:T(8,128)(2,1)}, bf16[768,384]{1,0:T(8,128)(2,1)}, u32[]{:S(2)}, u32[]{:S(2)}) collective-permute-start(bf16[768,384]{1,0:T(8,128)(2,1)} %broadcast_select_fusion), channel_id=1, source_target_pairs={{0,16},{16,0},{1,17},{17,1},{2,18},{18,2},{3,19},{19,3},{4,20},{20... | collective-permute-start | bytes 1769480 | tf_op jit(solution)/shard_map/ppermute | solution.py:169
  67.1 3.7 %shard_map.82 = (f32[3,768,1]{2,1,0:T(8,128)S(1)}, f32[3,768,256]{2,1,0:T(8,128)S(1)}) custom-call(s32[7]{0:T(128)S(1)} %stack.26.refs_0_, bf16[16,48,384]{2,1,0:T(8,128)(2,1)S(1)} %bitcast.94, bf16[768,384]{1,0:T(8,128)(2,1)S(1)} %copy-done.2, bf16[768,384]{1,0:T(8,128)(2,1)S(1)} %copy-done.1, bf16[768,384]{1,0:T(8,128)(2,1)S(1)} %copy-done.9, ...), custom_call_target="tpu_custom_call" | custom-call | flops 1811939328 | bytes 5898240 | tf_op jit(solution)/shard_map/pallas_call | solution.py:132
  70.8 6.9 %collective-permute-start.13 = (bf16[2,96,384]{2,1,0:T(8,128)(2,1)S(1)}, bf16[2,96,384]{2,1,0:T(8,128)(2,1)S(1)}, u32[]{:S(2)}, u32[]{:S(2)}) collective-permute-start(bf16[2,96,384]{2,1,0:T(8,128)(2,1)S(1)} %collective-permute-done.11.refs_3_), channel_id=1, source_target_pairs={{0,32},{32,64},{64,96},{96,128},{128,160},{160,192},{192,224},{224... | collective-permute-start | bytes 442376 | tf_op jit(solution)/shard_map/ppermute | solution.py:21
  77.7 6.6 %pad_maximum_fusion = bf16[768,6144]{1,0:T(8,128)(2,1)} fusion(bf16[384,6144]{1,0:T(8,128)(2,1)} %collective-permute-done.15, bf16[384,6144]{1,0:T(8,128)(2,1)S(1)} %copy-done.19), kind=kLoop, calls=%fused_computation | loop fusion | flops 18874368 | bytes 18874368 | tf_op jit(solution)/shard_map/concatenate | solution.py:211
  84.4 3.3 %collective-permute-start.16 = (bf16[2,96,384]{2,1,0:T(8,128)(2,1)S(1)}, bf16[2,96,384]{2,1,0:T(8,128)(2,1)}, u32[]{:S(2)}, u32[]{:S(2)}) collective-permute-start(bf16[2,96,384]{2,1,0:T(8,128)(2,1)S(1)} %collective-permute-done.13.refs_5_), channel_id=1, source_target_pairs={{0,32},{32,64},{64,96},{96,128},{128,160},{160,192},{192,224},{224... | collective-permute-start | bytes 442376 | tf_op jit(solution)/shard_map/ppermute | solution.py:21
  88.3 2.4 %collective-permute-done.16.refs_7_ = bf16[2,96,384]{2,1,0:T(8,128)(2,1)} collective-permute-done((bf16[2,96,384]{2,1,0:T(8,128)(2,1)S(1)}, bf16[2,96,384]{2,1,0:T(8,128)(2,1)}, u32[]{:S(2)}, u32[]{:S(2)}) %collective-permute-start.16) | collective-permute-done | bytes 147488 | tf_op jit(solution)/shard_map/ppermute | solution.py:21
  90.7 3.8 %collective-permute-start.18 = (bf16[2,96,384]{2,1,0:T(8,128)(2,1)}, bf16[2,96,384]{2,1,0:T(8,128)(2,1)}, u32[]{:S(2)}, u32[]{:S(2)}) collective-permute-start(bf16[2,96,384]{2,1,0:T(8,128)(2,1)} %collective-permute-done.16.refs_7_), channel_id=1, source_target_pairs={{0,32},{32,64},{64,96},{96,128},{128,160},{160,192},{192,224},{224... | collective-permute-start | bytes 442376 | tf_op jit(solution)/shard_map/ppermute | solution.py:21
  99.7 6.0 %shard_map.83 = (f32[3,768,1]{2,1,0:T(8,128)S(1)}, f32[3,768,256]{2,1,0:T(8,128)S(1)}) custom-call(s32[7]{0:T(128)S(1)} %stack.26.refs_0_, bf16[16,48,384]{2,1,0:T(8,128)(2,1)S(1)} %bitcast.95, bf16[768,384]{1,0:T(8,128)(2,1)S(1)} %copy-done.7, bf16[768,384]{1,0:T(8,128)(2,1)} %collective-permute-done.19.refs_3_, ...), custom_call_target="tpu_custom_call" | custom-call | flops 905969664 | bytes 5898240 | tf_op jit(solution)/shard_map/pallas_call | solution.py:132
  105.8 6.0 %shard_map.84 = bf16[768,384]{1,0:T(8,128)(2,1)S(1)} custom-call(s32[7]{0:T(128)S(1)} %stack.26.refs_0_, bf16[16,48,384]{2,1,0:T(8,128)(2,1)S(1)} %bitcast.96, bf16[2,96,384]{2,1,0:T(8,128)(2,1)S(1)} %broadcast_select_fusion.2.refs_2_, bf16[2,96,384]{2,1,0:T(8,128)(2,1)S(1)} %copy-done.13, bf16[2,96,384]{2,1,0:T(8,128)(2,1)S(1)} %copy-done.15, ...), custom_call_target="tpu_custom_call" | custom-call | flops 905969664 | bytes 5898240 | tf_op jit(solution)/shard_map/pallas_call | solution.py:132
  121.4 5.2 %collective-permute-done.26 = bf16[2,48,1728]{2,1,0:T(8,128)(2,1)S(1)} collective-permute-done((bf16[2,48,1728]{2,1,0:T(8,128)(2,1)S(1)}, bf16[2,48,1728]{2,1,0:T(8,128)(2,1)S(1)}, u32[]{:S(2)}, u32[]{:S(2)}) %collective-permute-start.26) | collective-permute-done | bytes 331808 | tf_op jit(solution)/shard_map/ppermute | solution.py:21
  131.3 12.2 %collective-permute-done.21 = bf16[4,48,2688]{2,1,0:T(8,128)(2,1)S(1)} collective-permute-done((bf16[4,48,2688]{2,1,0:T(8,128)(2,1)S(1)}, bf16[4,48,2688]{2,1,0:T(8,128)(2,1)S(1)}, u32[]{:S(2)}, u32[]{:S(2)}) %collective-permute-start.21) | collective-permute-done | bytes 1032224 | tf_op jit(solution)/shard_map/ppermute | solution.py:239
  149.8 3.3 %collective-permute-start.23 = (bf16[48,2688]{1,0:T(8,128)(2,1)S(1)}, bf16[48,2688]{1,0:T(8,128)(2,1)S(1)}, u32[]{:S(2)}, u32[]{:S(2)}) collective-permute-start(bf16[48,2688]{1,0:T(8,128)(2,1)S(1)} %pad_maximum_fusion.6), channel_id=1, source_target_pairs={{0,4},{4,8},{8,12},{12,0},{1,5},{5,9},{9,13},{13,1},{2,6},{6,10},{... | collective-permute-start | bytes 774152 | tf_op jit(solution)/shard_map/ppermute | solution.py:21
  153.1 2.7 %collective-permute-done.24 = bf16[48,1344]{1,0:T(8,128)(2,1)S(1)} collective-permute-done((bf16[48,1344]{1,0:T(8,128)(2,1)S(1)}, bf16[48,1344]{1,0:T(8,128)(2,1)S(1)}, u32[]{:S(2)}, u32[]{:S(2)}) %collective-permute-start.24) | collective-permute-done | bytes 129056 | tf_op jit(solution)/shard_map/ppermute | solution.py:21
  157.0 6.7 %collective-permute-done.25 = bf16[48,2688]{1,0:T(8,128)(2,1)S(1)} collective-permute-done((bf16[48,2688]{1,0:T(8,128)(2,1)S(1)}, bf16[48,2688]{1,0:T(8,128)(2,1)S(1)}, u32[]{:S(2)}, u32[]{:S(2)}) %collective-permute-start.25) | collective-permute-done | bytes 258080 | tf_op jit(solution)/shard_map/ppermute | solution.py:21
  (129 shorter events, 42.0 us)
Async XLA Ops:
  0.0 77.7 %collective-permute-start.15 = (bf16[384,6144]{1,0:T(8,128)(2,1)}, bf16[384,6144]{1,0:T(8,128)(2,1)}, u32[]{:S(2)}, u32[]{:S(2)}) collective-permute-start(bf16[384,6144]{1,0:T(8,128)(2,1)} %param.12), channel_id=1, source_target_pairs={{0,1},{1,0},{2,3},{3,2},{4,5},{5,4},{6,7},{7,6},{8,9},{9,8},{10,11... | collective-permute-start | bytes 14155784 | tf_op jit(solution)/shard_map/ppermute | solution.py:211
  1.3 6.9 %collective-permute-start = (bf16[2,96,384]{2,1,0:T(8,128)(2,1)S(1)}, bf16[2,96,384]{2,1,0:T(8,128)(2,1)S(1)}, u32[]{:S(2)}, u32[]{:S(2)}) collective-permute-start(bf16[2,96,384]{2,1,0:T(8,128)(2,1)S(1)} %get-tuple-element.55), channel_id=1, source_target_pairs={{0,32},{32,64},{64,96},{96,128},{128,160},{160,192},{192,224},{224... | collective-permute-start | bytes 442376 | tf_op jit(solution)/shard_map/ppermute | solution.py:21
  4.5 7.4 %collective-permute-start.2 = (bf16[2,96,384]{2,1,0:T(8,128)(2,1)S(1)}, bf16[2,96,384]{2,1,0:T(8,128)(2,1)S(1)}, u32[]{:S(2)}, u32[]{:S(2)}) collective-permute-start(bf16[2,96,384]{2,1,0:T(8,128)(2,1)S(1)} %get-tuple-element.54), channel_id=1, source_target_pairs={{0,224},{32,0},{64,32},{96,64},{128,96},{160,128},{192,160},{224,1... | collective-permute-start | bytes 442376 | tf_op jit(solution)/shard_map/ppermute | solution.py:21
  8.2 26.3 %collective-permute-start.5 = (bf16[768,384]{1,0:T(8,128)(2,1)S(1)}, bf16[768,384]{1,0:T(8,128)(2,1)S(1)}, u32[]{:S(2)}, u32[]{:S(2)}) collective-permute-start(bf16[768,384]{1,0:T(8,128)(2,1)S(1)} %copy-done.2), channel_id=1, source_target_pairs={{0,32},{32,64},{64,96},{96,128},{128,160},{160,192},{192,224},{224... | collective-permute-start | bytes 1769480 | tf_op jit(solution)/shard_map/ppermute | solution.py:21
  11.9 15.5 %collective-permute-start.1 = (bf16[2,96,384]{2,1,0:T(8,128)(2,1)S(1)}, bf16[2,96,384]{2,1,0:T(8,128)(2,1)}, u32[]{:S(2)}, u32[]{:S(2)}) collective-permute-start(bf16[2,96,384]{2,1,0:T(8,128)(2,1)S(1)} %get-tuple-element.53), channel_id=1, source_target_pairs={{0,32},{32,64},{64,96},{96,128},{128,160},{160,192},{192,224},{224... | collective-permute-start | bytes 442376 | tf_op jit(solution)/shard_map/ppermute | solution.py:21
  12.0 15.4 %collective-permute-start.3 = (bf16[2,96,384]{2,1,0:T(8,128)(2,1)S(1)}, bf16[2,96,384]{2,1,0:T(8,128)(2,1)S(1)}, u32[]{:S(2)}, u32[]{:S(2)}) collective-permute-start(bf16[2,96,384]{2,1,0:T(8,128)(2,1)S(1)} %get-tuple-element.52), channel_id=1, source_target_pairs={{0,224},{32,0},{64,32},{96,64},{128,96},{160,128},{192,160},{224,1... | collective-permute-start | bytes 442376 | tf_op jit(solution)/shard_map/ppermute | solution.py:21
  27.4 7.0 %collective-permute-start.4 = (bf16[2,96,384]{2,1,0:T(8,128)(2,1)S(1)}, bf16[2,96,384]{2,1,0:T(8,128)(2,1)S(1)}, u32[]{:S(2)}, u32[]{:S(2)}) collective-permute-start(bf16[2,96,384]{2,1,0:T(8,128)(2,1)S(1)} %bitcast_select_fusion.1), channel_id=1, source_target_pairs={{0,224},{32,0},{64,32},{96,64},{128,96},{160,128},{192,160},{224,1... | collective-permute-start | bytes 442376 | tf_op jit(solution)/shard_map/ppermute | solution.py:21
  35.5 14.8 %collective-permute-start.8 = (bf16[768,384]{1,0:T(8,128)(2,1)}, bf16[768,384]{1,0:T(8,128)(2,1)S(1)}, u32[]{:S(2)}, u32[]{:S(2)}) collective-permute-start(bf16[768,384]{1,0:T(8,128)(2,1)} %broadcast_select_fusion.1), channel_id=1, source_target_pairs={{0,16},{16,0},{1,17},{17,1},{2,18},{18,2},{3,19},{19,3},{4,20},{20... | collective-permute-start | bytes 1769480 | tf_op jit(solution)/shard_map/ppermute | solution.py:164
  41.0 16.9 %collective-permute-start.10 = (bf16[768,384]{1,0:T(8,128)(2,1)S(1)}, bf16[768,384]{1,0:T(8,128)(2,1)S(1)}, u32[]{:S(2)}, u32[]{:S(2)}) collective-permute-start(bf16[768,384]{1,0:T(8,128)(2,1)S(1)} %copy-done.1), channel_id=1, source_target_pairs={{0,32},{32,64},{64,96},{96,128},{128,160},{160,192},{192,224},{224... | collective-permute-start | bytes 1769480 | tf_op jit(solution)/shard_map/ppermute | solution.py:21
  58.0 12.8 %collective-permute-start.11 = (bf16[2,96,384]{2,1,0:T(8,128)(2,1)S(1)}, bf16[2,96,384]{2,1,0:T(8,128)(2,1)S(1)}, u32[]{:S(2)}, u32[]{:S(2)}) collective-permute-start(bf16[2,96,384]{2,1,0:T(8,128)(2,1)S(1)} %broadcast_select_fusion.2.refs_2_), channel_id=1, source_target_pairs={{0,32},{32,64},{64,96},{96,128},{128,160},{160,192},{192,224},{224... | collective-permute-start | bytes 442376 | tf_op jit(solution)/shard_map/ppermute | solution.py:21
  61.0 16.7 %collective-permute-start.12 = (bf16[2,96,384]{2,1,0:T(8,128)(2,1)S(1)}, bf16[2,96,384]{2,1,0:T(8,128)(2,1)S(1)}, u32[]{:S(2)}, u32[]{:S(2)}) collective-permute-start(bf16[2,96,384]{2,1,0:T(8,128)(2,1)S(1)} %broadcast_select_fusion.2.refs_2_), channel_id=1, source_target_pairs={{0,224},{32,0},{64,32},{96,64},{128,96},{160,128},{192,160},{224,1... | collective-permute-start | bytes 442376 | tf_op jit(solution)/shard_map/ppermute | solution.py:21
  61.9 35.1 %collective-permute-start.19 = (bf16[768,384]{1,0:T(8,128)(2,1)}, bf16[768,384]{1,0:T(8,128)(2,1)}, u32[]{:S(2)}, u32[]{:S(2)}) collective-permute-start(bf16[768,384]{1,0:T(8,128)(2,1)} %broadcast_select_fusion), channel_id=1, source_target_pairs={{0,16},{16,0},{1,17},{17,1},{2,18},{18,2},{3,19},{19,3},{4,20},{20... | collective-permute-start | bytes 1769480 | tf_op jit(solution)/shard_map/ppermute | solution.py:169
  70.8 13.5 %collective-permute-start.13 = (bf16[2,96,384]{2,1,0:T(8,128)(2,1)S(1)}, bf16[2,96,384]{2,1,0:T(8,128)(2,1)S(1)}, u32[]{:S(2)}, u32[]{:S(2)}) collective-permute-start(bf16[2,96,384]{2,1,0:T(8,128)(2,1)S(1)} %collective-permute-done.11.refs_3_), channel_id=1, source_target_pairs={{0,32},{32,64},{64,96},{96,128},{128,160},{160,192},{192,224},{224... | collective-permute-start | bytes 442376 | tf_op jit(solution)/shard_map/ppermute | solution.py:21
  77.7 10.6 %collective-permute-start.14 = (bf16[2,96,384]{2,1,0:T(8,128)(2,1)S(1)}, bf16[2,96,384]{2,1,0:T(8,128)(2,1)}, u32[]{:S(2)}, u32[]{:S(2)}) collective-permute-start(bf16[2,96,384]{2,1,0:T(8,128)(2,1)S(1)} %collective-permute-done.12.refs_4_), channel_id=1, source_target_pairs={{0,224},{32,0},{64,32},{96,64},{128,96},{160,128},{192,160},{224,1... | collective-permute-start | bytes 442376 | tf_op jit(solution)/shard_map/ppermute | solution.py:21
  88.3 17.5 %collective-permute-start.17 = (bf16[2,96,384]{2,1,0:T(8,128)(2,1)}, bf16[2,96,384]{2,1,0:T(8,128)(2,1)}, u32[]{:S(2)}, u32[]{:S(2)}) collective-permute-start(bf16[2,96,384]{2,1,0:T(8,128)(2,1)} %collective-permute-done.14.refs_6_), channel_id=1, source_target_pairs={{0,224},{32,0},{64,32},{96,64},{128,96},{160,128},{192,160},{224,1... | collective-permute-start | bytes 442376 | tf_op jit(solution)/shard_map/ppermute | solution.py:21
  90.7 15.0 %collective-permute-start.18 = (bf16[2,96,384]{2,1,0:T(8,128)(2,1)}, bf16[2,96,384]{2,1,0:T(8,128)(2,1)}, u32[]{:S(2)}, u32[]{:S(2)}) collective-permute-start(bf16[2,96,384]{2,1,0:T(8,128)(2,1)} %collective-permute-done.16.refs_7_), channel_id=1, source_target_pairs={{0,32},{32,64},{64,96},{96,128},{128,160},{160,192},{192,224},{224... | collective-permute-start | bytes 442376 | tf_op jit(solution)/shard_map/ppermute | solution.py:21
  116.4 10.2 %collective-permute-start.26 = (bf16[2,48,1728]{2,1,0:T(8,128)(2,1)S(1)}, bf16[2,48,1728]{2,1,0:T(8,128)(2,1)S(1)}, u32[]{:S(2)}, u32[]{:S(2)}) collective-permute-start(bf16[2,48,1728]{2,1,0:T(8,128)(2,1)S(1)} %get-tuple-element.59), channel_id=1, source_target_pairs={{0,4},{4,8},{8,12},{12,0},{1,5},{5,9},{9,13},{13,1},{2,6},{6,10},{... | collective-permute-start | bytes 995336 | tf_op jit(solution)/shard_map/ppermute | solution.py:21
  118.8 24.7 %collective-permute-start.21 = (bf16[4,48,2688]{2,1,0:T(8,128)(2,1)S(1)}, bf16[4,48,2688]{2,1,0:T(8,128)(2,1)S(1)}, u32[]{:S(2)}, u32[]{:S(2)}) collective-permute-start(bf16[4,48,2688]{2,1,0:T(8,128)(2,1)S(1)} %bitcast.101), channel_id=1, source_target_pairs={{0,2},{2,0},{1,3},{3,1},{4,6},{6,4},{5,7},{7,5},{8,10},{10,8},{9,1... | collective-permute-start | bytes 3096584 | tf_op jit(solution)/shard_map/ppermute | solution.py:239
  119.5 10.9 %collective-permute-start.28 = (bf16[2,48,1728]{2,1,0:T(8,128)(2,1)S(1)}, bf16[2,48,1728]{2,1,0:T(8,128)(2,1)S(1)}, u32[]{:S(2)}, u32[]{:S(2)}) collective-permute-start(bf16[2,48,1728]{2,1,0:T(8,128)(2,1)S(1)} %get-tuple-element.60), channel_id=1, source_target_pairs={{0,12},{4,0},{8,4},{12,8},{1,13},{5,1},{9,5},{13,9},{2,14},{6,2},{... | collective-permute-start | bytes 995336 | tf_op jit(solution)/shard_map/ppermute | solution.py:21
  126.9 18.7 %collective-permute-start.27 = (bf16[2,48,3456]{2,1,0:T(8,128)(2,1)S(1)}, bf16[2,48,3456]{2,1,0:T(8,128)(2,1)S(1)}, u32[]{:S(2)}, u32[]{:S(2)}) collective-permute-start(bf16[2,48,3456]{2,1,0:T(8,128)(2,1)S(1)} %pad_maximum_fusion.1), channel_id=1, source_target_pairs={{0,4},{4,8},{8,12},{12,0},{1,5},{5,9},{9,13},{13,1},{2,6},{6,10},{... | collective-permute-start | bytes 1990664 | tf_op jit(solution)/shard_map/ppermute | solution.py:21
  130.7 16.8 %collective-permute-start.29 = (bf16[2,48,3456]{2,1,0:T(8,128)(2,1)S(1)}, bf16[2,48,3456]{2,1,0:T(8,128)(2,1)S(1)}, u32[]{:S(2)}, u32[]{:S(2)}) collective-permute-start(bf16[2,48,3456]{2,1,0:T(8,128)(2,1)S(1)} %pad_maximum_fusion.2), channel_id=1, source_target_pairs={{0,12},{4,0},{8,4},{12,8},{1,13},{5,1},{9,5},{13,9},{2,14},{6,2},{... | collective-permute-start | bytes 1990664 | tf_op jit(solution)/shard_map/ppermute | solution.py:21
  147.7 8.5 %collective-permute-start.30 = (bf16[48,3456]{1,0:T(8,128)(2,1)S(1)}, bf16[48,3456]{1,0:T(8,128)(2,1)S(1)}, u32[]{:S(2)}, u32[]{:S(2)}) collective-permute-start(bf16[48,3456]{1,0:T(8,128)(2,1)S(1)} %fusion.5), channel_id=1, source_target_pairs={{0,2},{2,0},{1,3},{3,1},{4,6},{6,4},{5,7},{7,5},{8,10},{10,8},{9,1... | collective-permute-start | bytes 995336 | tf_op jit(solution)/shard_map/ppermute | solution.py:243
  149.8 7.1 %collective-permute-start.23 = (bf16[48,2688]{1,0:T(8,128)(2,1)S(1)}, bf16[48,2688]{1,0:T(8,128)(2,1)S(1)}, u32[]{:S(2)}, u32[]{:S(2)}) collective-permute-start(bf16[48,2688]{1,0:T(8,128)(2,1)S(1)} %pad_maximum_fusion.6), channel_id=1, source_target_pairs={{0,4},{4,8},{8,12},{12,0},{1,5},{5,9},{9,13},{13,1},{2,6},{6,10},{... | collective-permute-start | bytes 774152 | tf_op jit(solution)/shard_map/ppermute | solution.py:21
  156.1 7.6 %collective-permute-start.25 = (bf16[48,2688]{1,0:T(8,128)(2,1)S(1)}, bf16[48,2688]{1,0:T(8,128)(2,1)S(1)}, u32[]{:S(2)}, u32[]{:S(2)}) collective-permute-start(bf16[48,2688]{1,0:T(8,128)(2,1)S(1)} %pad_maximum_fusion.7), channel_id=1, source_target_pairs={{0,12},{4,0},{8,4},{12,8},{1,13},{5,1},{9,5},{13,9},{2,14},{6,2},{... | collective-permute-start | bytes 774152 | tf_op jit(solution)/shard_map/ppermute | solution.py:21
  (31 other events, 333.3 us)
